TPU v7x, 32 devices: a whole 2x2x4 slice. The times are simulated.
32 devices in a mesh: dp: 16 (over z, y, x), tensor: 2 (over core).
Axes of the slice: x: 2, y: 2, z: 4, core: 2. Of those that a mesh axis runs over, the one named last changes fastest.
Arguments:
- inputs: bfloat16 [16384, 1152], P(('dp', 'tensor')), may hold values from -6 to 6
- segments: int32 [16, 1024], P('dp'), may hold values from 0 to 2, as said below
- positions: int32 [16, 1024], P('dp'), may hold values from 0 to 5119, as said below
- query_weight: bfloat16 [1152, 1024], P('dp', 'tensor'), may hold values from -0.1875 to 0.1875
- key_weight: bfloat16 [1152, 256], P('dp'), may hold values from -0.1875 to 0.1875
- value_weight: bfloat16 [1152, 256], P('dp'), may hold values from -0.1875 to 0.1875
- output_weight: bfloat16 [1152, 1024], P('dp', 'tensor'), may hold values from -0.1875 to 0.1875
- gain_attn_in: bfloat16 [1152], P('dp'), may hold values from 0.099609375 to 1.8984375
- gain_attn_out: bfloat16 [1152], P('dp'), may hold values from 0.099609375 to 1.8984375
- gain_query: bfloat16 [256], P('dp'), may hold values from 0.099609375 to 1.8984375
- gain_key: bfloat16 [256], P('dp'), may hold values from 0.099609375 to 1.8984375
- gate_weight: bfloat16 [1152, 6912], P('dp', 'tensor'), may hold values from -0.1875 to 0.1875
- up_weight: bfloat16 [1152, 6912], P('dp', 'tensor'), may hold values from -0.1875 to 0.1875
- down_weight: bfloat16 [1152, 6912], P('dp', 'tensor'), may hold values from -0.078125 to 0.078125
- gain_ffn_in: bfloat16 [1152], P('dp'), may hold values from 0.099609375 to 1.8984375
- gain_ffn_out: bfloat16 [1152], P('dp'), may hold values from 0.099609375 to 1.8984375
- cotangent: bfloat16 [16384, 1152], P(('dp', 'tensor')), may hold values from -6 to 6
Outputs:
- layer_out: bfloat16 [16384, 1152], P(('dp', 'tensor'))
- input_grad: float32 [16384, 1152], P(('dp', 'tensor'))
- query_weight_grad: float32 [1152, 1024], P('dp', 'tensor')
- key_weight_grad: float32 [1152, 256], P(('dp', 'tensor'))
- value_weight_grad: float32 [1152, 256], P(('dp', 'tensor'))
- output_weight_grad: float32 [1152, 1024], P('dp', 'tensor')
- gain_attn_in_grad: float32 [1152], P(('dp', 'tensor'))
- gain_attn_out_grad: float32 [1152], P(('dp', 'tensor'))
- gain_query_grad: float32 [256], P(('dp', 'tensor'))
- gain_key_grad: float32 [256], P(('dp', 'tensor'))
- gate_weight_grad: float32 [1152, 6912], P('dp', 'tensor')
- up_weight_grad: float32 [1152, 6912], P('dp', 'tensor')
- down_weight_grad: float32 [1152, 6912], P('dp', 'tensor')
- gain_ffn_in_grad: float32 [1152], P(('dp', 'tensor'))
- gain_ffn_out_grad: float32 [1152], P(('dp', 'tensor'))
Inputs may be any that keep to these rules, and one draw needn't show every extreme that they name: `segments`: document numbers never fall along a sequence; each sequence holds documents 0, 1 and 2. Within a document positions rise by one from token to token; document 0 starts at 0; the last token of every sequence has position 5119.
All inputs are finite; a program needn't handle non-finite values.
Results may differ from a plain program's by a relative error of at most 0.02.
Values may be sent and summed in bfloat16 or wider, within the bound.
A program may use at most 256 MiB of HBM per device.

v0:
```python
import math

import jax
import jax.numpy as jnp
from jax import lax
from jax.sharding import PartitionSpec as P

WINDOW = 512


EPS = 1e-06
QUERY_SCALE = 0.0625
NEG_FILL = -1e30


def norm_rows(values, norm_gain):
    inv_rms = lax.rsqrt(jnp.mean(values * values, axis=-1, keepdims=True) + EPS)
    normed = values * inv_rms
    return (normed * norm_gain, normed, inv_rms)


def norm_back(gradient, normed, inv_rms, norm_gain):
    scaled_grad = gradient * norm_gain
    result = inv_rms * (
        scaled_grad - normed * jnp.mean(scaled_grad * normed, axis=-1, keepdims=True)
    )
    return (result, gradient * normed)


def rotary_tables(positions, width):
    freq_steps = jnp.arange(width // 2, dtype=jnp.float32) * (2.0 / width)
    inverse = jnp.exp(freq_steps * -math.log(10000.0))
    phases = positions.astype(jnp.float32)[:, None] * inverse[None, :]
    return (jnp.cos(phases), jnp.sin(phases))


def rotate(values, cosine, sine):
    half_width = values.shape[-1] // 2
    first_half = values[..., :half_width]
    second = values[..., half_width:]
    return jnp.concatenate(
        [first_half * cosine - second * sine, second * cosine + first_half * sine], axis=-1
    )


def gelu_product(gate_in, upper_in):
    return jax.nn.gelu(gate_in, approximate=True) * upper_in


def per_device(
    inputs,
    segments,
    positions,
    query_weight,
    key_weight,
    value_weight,
    output_weight,
    gain_attn_in,
    gain_attn_out,
    gain_query,
    gain_key,
    gate_weight,
    up_weight,
    down_weight,
    gain_ffn_in,
    gain_ffn_out,
    cotangent,
):
    half_rows = inputs.shape[0]
    offset = lax.axis_index("tensor") * half_rows
    (
        query_weight,
        key_weight,
        value_weight,
        output_weight,
        gain_attn_in,
        gain_attn_out,
        gain_query,
        gain_key,
    ) = (
        lax.all_gather(query_weight, "dp", axis=0, tiled=True),
        lax.all_gather(key_weight, "dp", axis=0, tiled=True),
        lax.all_gather(value_weight, "dp", axis=0, tiled=True),
        lax.all_gather(output_weight, "dp", axis=0, tiled=True),
        lax.all_gather(gain_attn_in, "dp", axis=0, tiled=True),
        lax.all_gather(gain_attn_out, "dp", axis=0, tiled=True),
        lax.all_gather(gain_query, "dp", axis=0, tiled=True),
        lax.all_gather(gain_key, "dp", axis=0, tiled=True),
    )
    gate_weight, up_weight, down_weight, gain_ffn_in, gain_ffn_out = (
        lax.all_gather(gate_weight, "dp", axis=0, tiled=True),
        lax.all_gather(up_weight, "dp", axis=0, tiled=True),
        lax.all_gather(down_weight, "dp", axis=0, tiled=True),
        lax.all_gather(gain_ffn_in, "dp", axis=0, tiled=True),
        lax.all_gather(gain_ffn_out, "dp", axis=0, tiled=True),
    )
    gain_attn_in = gain_attn_in.astype(jnp.float32)
    gain_attn_out = gain_attn_out.astype(jnp.float32)
    gain_query = gain_query.astype(jnp.float32)
    gain_key = gain_key.astype(jnp.float32)
    gain_ffn_in = gain_ffn_in.astype(jnp.float32)
    gain_ffn_out = gain_ffn_out.astype(jnp.float32)
    residual_in = inputs.astype(jnp.float32)
    attn_normed_in, attn_hat, attn_inv = norm_rows(residual_in, gain_attn_in)
    attn_local = attn_normed_in.astype(jnp.bfloat16)
    normed_rows = lax.all_gather(attn_local, "tensor", axis=0, tiled=True)
    seq_len = normed_rows.shape[0]
    head_dim = key_weight.shape[1]
    cosine, sine = rotary_tables(positions[0], head_dim)
    query_raw = jnp.dot(normed_rows, query_weight, preferred_element_type=jnp.float32)
    local_heads = query_raw.shape[1] // head_dim
    query_raw = query_raw.reshape(seq_len, local_heads, head_dim)
    key_raw = jnp.dot(normed_rows, key_weight, preferred_element_type=jnp.float32)
    value_low = jnp.dot(normed_rows, value_weight, preferred_element_type=jnp.float32).astype(
        jnp.bfloat16
    )
    query_normed, query_hat, query_inv = norm_rows(query_raw, gain_query)
    query_low = (rotate(query_normed, cosine[:, None, :], sine[:, None, :]) * QUERY_SCALE).astype(
        jnp.bfloat16
    )
    key_normed, key_hat, key_inv = norm_rows(key_raw, gain_key)
    key_low = rotate(key_normed, cosine, sine).astype(jnp.bfloat16)
    token_index = jnp.arange(seq_len)
    distance = token_index[:, None] - token_index[None, :]
    allowed = (segments[0][:, None] == segments[0][None, :]) & (distance >= 0) & (distance < WINDOW)
    scores = jnp.einsum("thd,sd->hts", query_low, key_low, preferred_element_type=jnp.float32)
    scores = jnp.where(allowed[None], scores, NEG_FILL)
    row_max = jnp.max(scores, axis=-1, keepdims=True)
    shifted = jnp.exp(scores - row_max)
    row_total = jnp.sum(shifted, axis=-1, keepdims=True)
    log_total = row_max + jnp.log(row_total)
    probs_low = (shifted / row_total).astype(jnp.bfloat16)
    context = jnp.einsum("hts,sd->thd", probs_low, value_low, preferred_element_type=jnp.float32)
    context = context.reshape(seq_len, local_heads * head_dim).astype(jnp.bfloat16)
    attn_terms = jnp.einsum("tc,dc->td", context, output_weight, preferred_element_type=jnp.float32)
    attn_branch = lax.psum_scatter(attn_terms, "tensor", scatter_dimension=0, tiled=True)
    post_attn, post_attn_hat, post_attn_inv = norm_rows(attn_branch, gain_attn_out)
    hidden_in = residual_in + post_attn
    ffn_normed, ffn_hat, ffn_inv = norm_rows(hidden_in, gain_ffn_in)
    ffn_inputs = lax.all_gather(ffn_normed.astype(jnp.bfloat16), "tensor", axis=0, tiled=True)
    gate_pre = jnp.dot(ffn_inputs, gate_weight, preferred_element_type=jnp.float32)
    upper_pre = jnp.dot(ffn_inputs, up_weight, preferred_element_type=jnp.float32)
    activated, gelu_pull = jax.vjp(gelu_product, gate_pre, upper_pre)
    hidden_low = activated.astype(jnp.bfloat16)
    ffn_terms = jnp.einsum("tf,df->td", hidden_low, down_weight, preferred_element_type=jnp.float32)
    ffn_branch = lax.psum_scatter(ffn_terms, "tensor", scatter_dimension=0, tiled=True)
    post_ffn, post_ffn_hat, post_ffn_inv = norm_rows(ffn_branch, gain_ffn_out)
    layer_out = (hidden_in + post_ffn).astype(jnp.bfloat16)
    out_grad = cotangent.astype(jnp.float32)
    ffn_branch_grad, gain_ffn_out_rows = norm_back(
        out_grad, post_ffn_hat, post_ffn_inv, gain_ffn_out
    )
    ffn_grad_all = lax.all_gather(
        ffn_branch_grad.astype(jnp.bfloat16), "tensor", axis=0, tiled=True
    )
    down_weight_grad = jnp.einsum(
        "td,tf->df", ffn_grad_all, hidden_low, preferred_element_type=jnp.float32
    )
    hidden_grad = jnp.dot(ffn_grad_all, down_weight, preferred_element_type=jnp.float32)
    gate_grad, upper_grad = gelu_pull(hidden_grad)
    gate_low = gate_grad.astype(jnp.bfloat16)
    upper_low = upper_grad.astype(jnp.bfloat16)
    gate_weight_grad = jnp.einsum(
        "td,tf->df", ffn_inputs, gate_low, preferred_element_type=jnp.float32
    )
    up_weight_grad = jnp.einsum(
        "td,tf->df", ffn_inputs, upper_low, preferred_element_type=jnp.float32
    )
    ffn_in_terms = jnp.einsum(
        "tf,df->td", gate_low, gate_weight, preferred_element_type=jnp.float32
    ) + jnp.einsum("tf,df->td", upper_low, up_weight, preferred_element_type=jnp.float32)
    ffn_in_grad = lax.psum_scatter(ffn_in_terms, "tensor", scatter_dimension=0, tiled=True)
    ffn_norm_grad, gain_ffn_in_rows = norm_back(ffn_in_grad, ffn_hat, ffn_inv, gain_ffn_in)
    hidden_total = out_grad + ffn_norm_grad
    attn_branch_grad, gain_attn_out_rows = norm_back(
        hidden_total, post_attn_hat, post_attn_inv, gain_attn_out
    )
    branch_all = lax.all_gather(attn_branch_grad.astype(jnp.bfloat16), "tensor", axis=0, tiled=True)
    output_weight_grad = jnp.einsum(
        "td,tc->dc", branch_all, context, preferred_element_type=jnp.float32
    )
    context_grad = jnp.dot(branch_all, output_weight, preferred_element_type=jnp.float32)
    context_grad = context_grad.reshape(seq_len, local_heads, head_dim).astype(jnp.bfloat16)
    scores = jnp.einsum("thd,sd->hts", query_low, key_low, preferred_element_type=jnp.float32)
    scores = jnp.where(allowed[None], scores, NEG_FILL)
    probs = jnp.exp(scores - log_total)
    prob_grad = jnp.einsum(
        "thd,sd->hts", context_grad, value_low, preferred_element_type=jnp.float32
    )
    row_inner = jnp.sum(prob_grad * probs, axis=-1, keepdims=True)
    score_grad = (probs * (prob_grad - row_inner)).astype(jnp.bfloat16)
    value_grad = jnp.einsum(
        "hts,thd->sd", probs.astype(jnp.bfloat16), context_grad, preferred_element_type=jnp.float32
    )
    query_grad = (
        jnp.einsum("hts,sd->thd", score_grad, key_low, preferred_element_type=jnp.float32)
        * QUERY_SCALE
    )
    key_grad = jnp.einsum("hts,thd->sd", score_grad, query_low, preferred_element_type=jnp.float32)
    query_turned = rotate(query_grad, cosine[:, None, :], -sine[:, None, :])
    query_raw_grad, gain_query_parts = norm_back(query_turned, query_hat, query_inv, gain_query)
    gain_query_grad = jnp.sum(gain_query_parts, axis=(0, 1))
    query_raw_low = query_raw_grad.reshape(seq_len, local_heads * head_dim).astype(jnp.bfloat16)
    query_weight_grad = jnp.einsum(
        "td,tc->dc", normed_rows, query_raw_low, preferred_element_type=jnp.float32
    )
    input_terms = jnp.einsum(
        "tc,dc->td", query_raw_low, query_weight, preferred_element_type=jnp.float32
    )
    input_part, key_part, value_part = (
        lax.psum_scatter(
            input_terms.astype(jnp.bfloat16), "tensor", scatter_dimension=0, tiled=True
        ).astype(jnp.float32),
        lax.psum_scatter(
            key_grad.astype(jnp.bfloat16), "tensor", scatter_dimension=0, tiled=True
        ).astype(jnp.float32),
        lax.psum_scatter(
            value_grad.astype(jnp.bfloat16), "tensor", scatter_dimension=0, tiled=True
        ).astype(jnp.float32),
    )
    local_cos = lax.dynamic_slice_in_dim(cosine, offset, half_rows, 0)
    local_sin = lax.dynamic_slice_in_dim(sine, offset, half_rows, 0)
    local_key_hat = lax.dynamic_slice_in_dim(key_hat, offset, half_rows, 0)
    local_key_inv = lax.dynamic_slice_in_dim(key_inv, offset, half_rows, 0)
    key_turned = rotate(key_part, local_cos, -local_sin)
    key_raw_grad, gain_key_rows = norm_back(key_turned, local_key_hat, local_key_inv, gain_key)
    key_raw_low = key_raw_grad.astype(jnp.bfloat16)
    value_raw_low = value_part.astype(jnp.bfloat16)
    key_weight_grad = jnp.einsum(
        "td,tc->dc", attn_local, key_raw_low, preferred_element_type=jnp.float32
    )
    value_weight_grad = jnp.einsum(
        "td,tc->dc", attn_local, value_raw_low, preferred_element_type=jnp.float32
    )
    normed_grad = (
        input_part
        + jnp.einsum("tc,dc->td", key_raw_low, key_weight, preferred_element_type=jnp.float32)
        + jnp.einsum("tc,dc->td", value_raw_low, value_weight, preferred_element_type=jnp.float32)
    )
    input_back, gain_attn_in_rows = norm_back(normed_grad, attn_hat, attn_inv, gain_attn_in)
    input_grad = hidden_total + input_back
    query_weight_grad, output_weight_grad, gate_weight_grad, up_weight_grad, down_weight_grad = (
        lax.psum_scatter(query_weight_grad, "dp", scatter_dimension=0, tiled=True),
        lax.psum_scatter(output_weight_grad, "dp", scatter_dimension=0, tiled=True),
        lax.psum_scatter(gate_weight_grad, "dp", scatter_dimension=0, tiled=True),
        lax.psum_scatter(up_weight_grad, "dp", scatter_dimension=0, tiled=True),
        lax.psum_scatter(down_weight_grad, "dp", scatter_dimension=0, tiled=True),
    )
    shared = (
        lax.psum_scatter(key_weight_grad, ("dp", "tensor"), scatter_dimension=0, tiled=True),
        lax.psum_scatter(value_weight_grad, ("dp", "tensor"), scatter_dimension=0, tiled=True),
        lax.psum_scatter(
            jnp.sum(gain_attn_in_rows, axis=0), ("dp", "tensor"), scatter_dimension=0, tiled=True
        ),
        lax.psum_scatter(
            jnp.sum(gain_attn_out_rows, axis=0), ("dp", "tensor"), scatter_dimension=0, tiled=True
        ),
        lax.psum_scatter(gain_query_grad, ("dp", "tensor"), scatter_dimension=0, tiled=True),
        lax.psum_scatter(
            jnp.sum(gain_key_rows, axis=0), ("dp", "tensor"), scatter_dimension=0, tiled=True
        ),
        lax.psum_scatter(
            jnp.sum(gain_ffn_in_rows, axis=0), ("dp", "tensor"), scatter_dimension=0, tiled=True
        ),
        lax.psum_scatter(
            jnp.sum(gain_ffn_out_rows, axis=0), ("dp", "tensor"), scatter_dimension=0, tiled=True
        ),
    )
    (
        key_weight_grad,
        value_weight_grad,
        gain_attn_in_grad,
        gain_attn_out_grad,
        gain_query_grad,
        gain_key_grad,
        gain_ffn_in_grad,
        gain_ffn_out_grad,
    ) = shared
    return (
        layer_out,
        input_grad,
        query_weight_grad,
        key_weight_grad,
        value_weight_grad,
        output_weight_grad,
        gain_attn_in_grad,
        gain_attn_out_grad,
        gain_query_grad,
        gain_key_grad,
        gate_weight_grad,
        up_weight_grad,
        down_weight_grad,
        gain_ffn_in_grad,
        gain_ffn_out_grad,
    )


def solution(mesh):
    in_specs = (
        P(("dp", "tensor"), None),
        P("dp", None),
        P("dp", None),
        P("dp", "tensor"),
        P("dp", None),
        P("dp", None),
        P("dp", "tensor"),
        P("dp"),
        P("dp"),
        P("dp"),
        P("dp"),
        P("dp", "tensor"),
        P("dp", "tensor"),
        P("dp", "tensor"),
        P("dp"),
        P("dp"),
        P(("dp", "tensor"), None),
    )
    out_specs = (
        P(("dp", "tensor"), None),
        P(("dp", "tensor"), None),
        P("dp", "tensor"),
        P(("dp", "tensor"), None),
        P(("dp", "tensor"), None),
        P("dp", "tensor"),
        P(("dp", "tensor")),
        P(("dp", "tensor")),
        P(("dp", "tensor")),
        P(("dp", "tensor")),
        P("dp", "tensor"),
        P("dp", "tensor"),
        P("dp", "tensor"),
        P(("dp", "tensor")),
        P(("dp", "tensor")),
    )
    return jax.shard_map(
        per_device, mesh=mesh, in_specs=in_specs, out_specs=out_specs, check_vma=False
    )
```

profile of v0, /device:TPU:0, one launch (start us, length us, event | category | flops | bytes accessed | tf_op | source)
XLA Modules:
  0.0 1834.5 jit_solution(13904170096414140423)
XLA Ops:
  16.5 78.6 %all-reduce.20 = (bf16[1152]{0:T(1024)(128)(2,1)S(1)}, bf16[256]{0:T(256)(128)(2,1)S(1)}, bf16[256]{0:T(256)(128)(2,1)S(1)}, bf16[1152]{0:T(1024)(128)(2,1)S(1)}...) all-reduce(bf16[1152]{0:T(1024)(128)(2,1)S(1)} %dynamic-update-slice, ...), channel_id=1, replica_groups=mesh['dp'=16,'tensor'=2] {'dp'}, use_global_device_ids=true, to_apply=%add | all-reduce | flops 5120 | bytes 20480
  95.7 2.7 fusion.34
  100.1 39.3 %all_gather.54 = bf16[1152,256]{1,0:T(8,128)(2,1)S(1)} all-gather(bf16[72,256]{1,0:T(8,128)(2,1)S(1)} %copy-done.48), channel_id=1, replica_groups=mesh['dp'=16,'tensor'=2] {'dp'}, dimensions={0}, use_global_device_ids=true | all-gather | bytes 626688 | tf_op jit(solution)/shard_map/all_gather | solution.py:82
  139.3 45.2 %all_gather.53 = bf16[1152,256]{1,0:T(8,128)(2,1)} all-gather(bf16[72,256]{1,0:T(8,128)(2,1)S(1)} %copy-done.49), channel_id=1, replica_groups=mesh['dp'=16,'tensor'=2] {'dp'}, dimensions={0}, use_global_device_ids=true | all-gather | bytes 626688 | tf_op jit(solution)/shard_map/all_gather | solution.py:83
  186.3 2.9 multiply_reduce_fusion.9
  190.3 3.1 fusion.55
  195.6 4.9 multiply_reduce_fusion.8
  211.5 3.0 fusion.46
  214.5 10.1 all-gather.14.cloned.1.call-done
  224.7 5.0 fusion.74
  230.4 11.0 reduce-scatter.22.cloned.1.call-done
  247.9 10.1 all-gather.16.cloned.1.call-done
  258.0 113.1 %all-gather.18.cloned.1.call-done = bf16[1152,3456]{1,0:T(8,128)(2,1)} async-done(((bf16[72,3456]{1,0:T(8,128)(2,1)}), bf16[1152,3456]{1,0:T(8,128)(2,1)}) %all-gather.18.cloned.1.call-update) | async-done | bytes 7962640 | tf_op jit(solution)/shard_map/all_gather | solution.py:91
  371.1 15.6 fusion.75
  386.7 94.7 %all-gather.20.cloned.1.call-done = bf16[1152,3456]{1,0:T(8,128)(2,1)} async-done(((bf16[72,3456]{1,0:T(8,128)(2,1)}), bf16[1152,3456]{1,0:T(8,128)(2,1)}) %all-gather.20.cloned.1.call-update) | async-done | bytes 7962640 | tf_op jit(solution)/shard_map/all_gather | solution.py:92
  481.4 19.7 %multiply_convert_fusion.1 = (bf16[1024,3456]{1,0:T(8,128)(2,1)}, f32[1024,3456]{1,0:T(8,128)}) fusion(f32[1024,3456]{1,0:T(8,128)} %fusion.75, bf16[1024,1152]{1,0:T(8,128)(2,1)} %all-gather.16.cloned.1.call-done, bf16[1152,3456]{1,0:T(8,128)(2,1)} %all-gather.20.cloned.1.call-done), kind=kOutput, calls=%fused_computation.10 | convolution fusion | flops 8189116416 | bytes 45711360 | tf_op jit(solution)/shard_map/dot_general | solution.py:142
  501.2 90.5 %all-gather.22.cloned.1.call-done = bf16[1152,3456]{1,0:T(8,128)(2,1)} async-done(((bf16[72,3456]{1,0:T(8,128)(2,1)}), bf16[1152,3456]{1,0:T(8,128)(2,1)}) %all-gather.22.cloned.1.call-update) | async-done | bytes 7962640 | tf_op jit(solution)/shard_map/all_gather | solution.py:93
  591.7 15.6 fusion.76
  609.0 9.3 reduce-scatter.24.cloned.1.call-done
  625.0 12.2 all-gather.24.cloned.1.call-done
  637.2 25.1 %multiply_convert_fusion = (bf16[1024,3456]{1,0:T(8,128)(2,1)}, bf16[1024,3456]{1,0:T(8,128)(2,1)S(1)}) fusion(f32[1024,3456]{1,0:T(8,128)} %fusion.75, f32[1024,3456]{1,0:T(8,128)} %get-tuple-element.74, bf16[1024,1152]{1,0:T(8,128)(2,1)} %all-gather.24.cloned.1.call-done, bf16[1152,3456]{1,0:T(8,128)(2,1)} %all-gather.22.cloned.1.call-done), kind=kOutput, calls=%fused_computation.9 | convolution fusion | flops 8238661632 | bytes 52789248 | tf_op jit(solution)/shard_map/dot_general | solution.py:159
  662.3 17.1 fusion.77
  679.4 16.3 convolution_add_fusion
  696.0 13.7 reduce-scatter.26.cloned.1.call-done
  709.7 3.0 multiply_reduce_fusion
  718.0 11.9 all-gather.26.cloned.1.call-done
  730.0 3.5 convolution_convert_fusion.1
  733.6 5.3 fusion.9
  739.8 2.6 fusion.11
  746.7 5.3 multiply_bitcast_fusion
  752.0 6.2 fusion.50
  762.4 3.0 copy.71
  767.8 3.0 convolution_convert_fusion
  772.5 4.1 fusion.81
  778.4 2.8 fusion.78
  783.0 14.5 fusion.84
  799.2 14.6 fusion.83
  814.0 14.7 fusion.82
  832.2 2.6 fusion.80
  834.8 84.6 %fusion.73 = (f32[40,256]{1,0:T(8,128)S(1)}, f32[40,256]{1,0:T(8,128)S(1)}) fusion(f32[1152,256]{1,0:T(8,128)S(1)} %fusion.79, f32[1152,256]{1,0:T(8,128)} %fusion.80), kind=kCustom, calls=%all-reduce-scatter.2 | all-reduce-scatter fusion | flops 655361 | bytes 2441216
  928.5 4.1 collective-permute-start.7
  937.6 4.2 fusion.39
  941.8 48.8 %all-reduce.19 = (f32[1152]{0:T(1024)}, f32[1152]{0:T(1024)}, f32[256]{0:T(256)}, f32[256]{0:T(256)}, f32[1152]{0:T(1024)}, /*index=5*/f32[1152]{0:T(1024)}) all-reduce(f32[1152]{0:T(1024)} %get-tuple-element.21, f32[1152]{0:T(1024)} %get-tuple-element.17, ...), channel_id=12, replica_groups=mesh['dp'=16,'tensor'=2] {'dp','tensor'}, use_global_device_ids=true, to_apply=%region_26.27.clone | all-reduce | flops 5120 | bytes 40960
  998.9 3.7 fusion.38
  1002.6 50.4 %reduce-scatter.34.cloned.1.call-done = f32[72,512]{1,0:T(8,128)} async-done(((f32[1152,512]{1,0:T(8,128)}), f32[72,512]{1,0:T(8,128)}) %reduce-scatter.34.cloned.1.call-update) | async-done | bytes 147472 | tf_op jit(solution)/shard_map/reduce_scatter | solution.py:243
  1053.0 257.7 %reduce-scatter.42.cloned.1.call-done = f32[72,3456]{1,0:T(8,128)} async-done(((f32[1152,3456]{1,0:T(8,128)}), f32[72,3456]{1,0:T(8,128)}) %reduce-scatter.42.cloned.1.call-update) | async-done | bytes 995344
  1310.7 258.4 %reduce-scatter.40.cloned.1.call-done = f32[72,3456]{1,0:T(8,128)} async-done(((f32[1152,3456]{1,0:T(8,128)}), f32[72,3456]{1,0:T(8,128)}) %reduce-scatter.40.cloned.1.call-update) | async-done | bytes 995344
  1569.2 258.3 %reduce-scatter.38.cloned.1.call-done = f32[72,3456]{1,0:T(8,128)} async-done(((f32[1152,3456]{1,0:T(8,128)}), f32[72,3456]{1,0:T(8,128)}) %reduce-scatter.38.cloned.1.call-update) | async-done | bytes 995344
  (297 shorter events, 91.1 us)
Async XLA Ops:
  7.2 179.1 %all-gather.10.cloned.1.call-start = ((), (), s32[]{:S(2)}) async-start(), calls=%async_computation.11 | async-start | bytes 3538944 | tf_op jit(solution)/shard_map/all_gather | solution.py:106
  9.8 90.2 %copy-start.68 = (s32[1,1024]{1,0:T(1,128)S(1)}, s32[1,1024]{1,0:T(1,128)}, u32[]{:S(2)}) copy-start(s32[1,1024]{1,0:T(1,128)} %param.19) | copy-start | bytes 12292
  9.8 90.2 %copy-start.48 = (bf16[72,256]{1,0:T(8,128)(2,1)S(1)}, bf16[72,256]{1,0:T(8,128)(2,1)}, u32[]{:S(2)}) copy-start(bf16[72,256]{1,0:T(8,128)(2,1)} %param.21) | copy-start | bytes 110596
  11.4 127.9 %copy-start.49 = (bf16[72,256]{1,0:T(8,128)(2,1)S(1)}, bf16[72,256]{1,0:T(8,128)(2,1)}, u32[]{:S(2)}) copy-start(bf16[72,256]{1,0:T(8,128)(2,1)} %param.22) | copy-start | bytes 110596
  11.4 173.2 %copy-start.57 = (f32[512]{0:T(512)}, f32[512]{0:T(512)S(1)}, u32[]{:S(2)}) copy-start(f32[512]{0:T(512)S(1)} %add_rsqrt_fusion.5) | copy-start | bytes 6148
  95.7 88.8 %copy-start.62 = (s32[1,1024]{1,0:T(1,128)S(1)}, s32[1,1024]{1,0:T(1,128)}, u32[]{:S(2)}) copy-start(s32[1,1024]{1,0:T(1,128)} %param.18) | copy-start | bytes 12292
  98.4 97.2 %all-gather.12.cloned.1.call-start = ((), (), s32[]{:S(2)}) async-start(), calls=%async_computation.12 | async-start | bytes 1253376 | tf_op jit(solution)/shard_map/all_gather | solution.py:81
  99.2 125.5 %all-gather.14.cloned.1.call-start = ((), (), s32[]{:S(2)}) async-start(), calls=%async_computation.13 | async-start | bytes 1253376 | tf_op jit(solution)/shard_map/all_gather | solution.py:84
  99.9 141.5 %reduce-scatter.22.cloned.1.call-start = ((), (), s32[]{:S(2)}) async-start(), calls=%async_computation.14 | async-start | bytes 7077888 | tf_op jit(solution)/shard_map/reduce_scatter | solution.py:136
  100.0 89.2 %copy-start.63 = (f32[256]{0:T(256)}, f32[256]{0:T(256)S(1)}, u32[]{:S(2)}) copy-start(f32[256]{0:T(256)S(1)} %convert_element_type.116) | copy-start | bytes 3076
  100.0 102.4 %copy-start.65 = (f32[256]{0:T(256)}, f32[256]{0:T(256)S(1)}, u32[]{:S(2)}) copy-start(f32[256]{0:T(256)S(1)} %convert_element_type.119) | copy-start | bytes 3076
  139.3 49.9 %copy-start.16 = (bf16[1152,256]{1,0:T(8,128)(2,1)}, bf16[1152,256]{1,0:T(8,128)(2,1)S(1)}, u32[]{:S(2)}) copy-start(bf16[1152,256]{1,0:T(8,128)(2,1)S(1)} %all_gather.54) | copy-start | bytes 1769476
  186.2 23.8 %copy-start.5 = (pred[1024,1024]{0,1:T(8,128)(4,1)}, pred[1024,1024]{0,1:T(8,128)(4,1)S(1)}, u32[]{:S(2)}) copy-start(pred[1024,1024]{0,1:T(8,128)(4,1)S(1)} %fusion.22) | copy-start | bytes 3145732
  193.4 7.1 copy-start.22
  193.4 7.1 copy-start.24
  193.4 11.3 copy-start.39
  214.5 15.2 copy-start.73
  229.7 13.7 copy-start.3
  229.7 28.3 %all-gather.16.cloned.1.call-start = ((), (), s32[]{:S(2)}) async-start(), calls=%async_computation.15 | async-start | bytes 3538944 | tf_op jit(solution)/shard_map/all_gather | solution.py:140
  245.8 125.4 %all-gather.18.cloned.1.call-start = ((), (), s32[]{:S(2)}) async-start(), calls=%async_computation.16 | async-start | bytes 8460288 | tf_op jit(solution)/shard_map/all_gather | solution.py:91
  246.3 235.1 %all-gather.20.cloned.1.call-start = ((), (), s32[]{:S(2)}) async-start(), calls=%async_computation.17 | async-start | bytes 8460288 | tf_op jit(solution)/shard_map/all_gather | solution.py:92
  247.1 344.6 %all-gather.22.cloned.1.call-start = ((), (), s32[]{:S(2)}) async-start(), calls=%async_computation.18 | async-start | bytes 8460288 | tf_op jit(solution)/shard_map/all_gather | solution.py:93
  247.8 370.5 %reduce-scatter.24.cloned.1.call-start = ((), (), s32[]{:S(2)}) async-start(), calls=%async_computation.19 | async-start | bytes 7077888 | tf_op jit(solution)/shard_map/reduce_scatter | solution.py:146
  607.3 13.1 copy-start.13
  607.3 29.9 %all-gather.24.cloned.1.call-start = ((), (), s32[]{:S(2)}) async-start(), calls=%async_computation.20 | async-start | bytes 3538944 | tf_op jit(solution)/shard_map/all_gather | solution.py:153
  625.0 84.7 %reduce-scatter.26.cloned.1.call-start = ((), (), s32[]{:S(2)}) async-start(), calls=%async_computation.21 | async-start | bytes 7077888 | tf_op jit(solution)/shard_map/reduce_scatter | solution.py:172
  662.3 17.1 copy-start.74
  695.8 34.2 %all-gather.26.cloned.1.call-start = ((), (), s32[]{:S(2)}) async-start(), calls=%async_computation.22 | async-start | bytes 3538944 | tf_op jit(solution)/shard_map/all_gather | solution.py:178
  717.7 111.8 %reduce-scatter.30.cloned.1.call-start = ((), (), s32[]{:S(2)}) async-start(), calls=%async_computation.24 | async-start | bytes 786432 | tf_op jit(solution)/shard_map/reduce_scatter | solution.py:214
  718.0 15.5 copy-start.6
  718.0 15.5 copy-start.38
  746.6 85.6 %reduce-scatter.32.cloned.1.call-start = ((), (), s32[]{:S(2)}) async-start(), calls=%async_computation.25 | async-start | bytes 786432 | tf_op jit(solution)/shard_map/reduce_scatter | solution.py:217
  758.2 177.5 %reduce-scatter.28.cloned.1.call-start = ((), (), s32[]{:S(2)}) async-start(), calls=%async_computation.23 | async-start | bytes 3538944 | tf_op jit(solution)/shard_map/reduce_scatter | solution.py:211
  770.8 231.8 %reduce-scatter.36.cloned.1.call-start = ((), (), s32[]{:S(2)}) async-start(), calls=%async_computation.27 | async-start | bytes 2506752 | tf_op jit(solution)/shard_map/reduce_scatter | solution.py:244
  776.6 276.4 %reduce-scatter.34.cloned.1.call-start = ((), (), s32[]{:S(2)}) async-start(), calls=%async_computation.26 | async-start | bytes 2506752 | tf_op jit(solution)/shard_map/reduce_scatter | solution.py:243
  781.2 529.5 %reduce-scatter.42.cloned.1.call-start = ((), (), s32[]{:S(2)}) async-start(), calls=%async_computation.30 | async-start | bytes 16920576
  797.5 771.6 %reduce-scatter.40.cloned.1.call-start = ((), (), s32[]{:S(2)}) async-start(), calls=%async_computation.29 | async-start | bytes 16920576
  813.8 1013.6 %reduce-scatter.38.cloned.1.call-start = ((), (), s32[]{:S(2)}) async-start(), calls=%async_computation.28 | async-start | bytes 16920576
  832.2 103.6 %copy-start.17 = (bf16[1152,256]{1,0:T(8,128)(2,1)S(1)}, bf16[1152,256]{1,0:T(8,128)(2,1)}, u32[]{:S(2)}) copy-start(bf16[1152,256]{1,0:T(8,128)(2,1)} %copy-done.16) | copy-start | bytes 1769476
  919.3 7.8 collective-permute-start.2
  920.6 7.8 collective-permute-start.1
  921.9 3.9 collective-permute-start.3
  923.2 10.0 collective-permute-start
  924.5 9.4 collective-permute-start.6
  925.9 8.1 collective-permute-start.5
  927.2 6.8 collective-permute-start.4
  928.5 5.4 collective-permute-start.7
  937.6 61.3 %copy-start.8 = (f32[512,1152]{1,0:T(8,128)S(1)}, f32[512,1152]{1,0:T(8,128)}, u32[]{:S(2)}) copy-start(f32[512,1152]{1,0:T(8,128)} %copy-done.7) | copy-start | bytes 7077892
  (57 other events, 146.0 us)
Sparse Core Ops, SparseCore 0:
  98.6 6.8 all-gather.9
  108.2 58.6 all-gather.11
  169.7 54.9 all-gather.13
  229.8 11.4 reduce-scatter.21
  245.9 12.1 all-gather.15
  260.9 110.1 all-gather.17
  374.2 107.1 all-gather.19
  484.5 107.1 all-gather.21
  607.5 10.7 reduce-scatter.23
  625.1 12.1 all-gather.23
  695.9 13.7 reduce-scatter.25
  717.8 12.1 all-gather.25
  746.7 9.1 reduce-scatter.29
  758.3 9.1 reduce-scatter.31
  770.9 11.0 reduce-scatter.27
  787.4 132.6 reduce-scatter.35
  926.2 126.7 reduce-scatter.33
  1059.2 251.4 reduce-scatter.41
  1317.1 252.0 reduce-scatter.39
  1575.4 251.9 reduce-scatter.37
where the time goes:
time: 1840 us; the launch traced here: 1830 us
  waiting for transfers between devices  1210 us (66%)
  blocking collectives  297 us (16%)
  matrix products  213 us (12%)
  other arithmetic  46.3 us (3%)
  local copies, waits for them, and re-layouts  40.6 us (2%)
    unnamed x31, waiting for transfers between devices  778 us
    unnamed x3, blocking collectives  212 us
    all_gather x1, waiting for transfers between devices, per_device(): lax.all_gather(gate_weight, 'dp', axis=0, tiled=True)  113 us
    all_gather x1, waiting for transfers between devices, per_device(): lax.all_gather(up_weight, 'dp', axis=0, tiled=True)  94.7 us
    all_gather x1, waiting for transfers between devices, per_device(): lax.all_gather(down_weight, 'dp', axis=0, tiled=True)  90.5 us
    reduce_scatter x1, waiting for transfers between devices, per_device(): lax.psum_scatter(query_weight_grad, 'dp', scatter_dimension=0, tiled=True)  50.4 us
    all_gather x1, blocking collectives, per_device(): lax.all_gather(value_weight, 'dp', axis=0, tiled=True)  45.2 us
    all_gather x1, blocking collectives, per_device(): lax.all_gather(key_weight, 'dp', axis=0, tiled=True)  39.3 us
  transfers between devices with their start and end apart: 28, of which 15 were waited for; matrix products, arithmetic and copies ran while one was open for 14% of the time, Pallas kernels for 0%

commit v1 on v0

--- a/solution.py
+++ b/solution.py
@@ -45,6 +45,68 @@
 
 def gelu_product(gate_in, upper_in):
     return jax.nn.gelu(gate_in, approximate=True) * upper_in
+
+
+def swap_pair(values):
+    return lax.ppermute(values, "tensor", [(0, 1), (1, 0)])
+
+
+def pair_rows(own):
+    return jnp.concatenate([own, swap_pair(own)], axis=0)
+
+
+def pair_sum(terms):
+    half = terms.shape[0] // 2
+    return terms[:half] + swap_pair(terms[half:].astype(jnp.bfloat16)).astype(jnp.float32)
+
+
+def halving_sum(terms, order):
+    count = lax.axis_size("dp")
+    place = lax.axis_index("dp")
+    bits = len(order)
+    rows = terms.shape[0] // count
+    total = terms.reshape((2,) * bits + (rows, terms.shape[1]))
+    for bit in order:
+        axis = bits - 1 - bit
+        mine = (place >> bit) & 1
+        kept = lax.dynamic_slice_in_dim(total, mine, 1, axis)
+        sent = lax.dynamic_slice_in_dim(total, 1 - mine, 1, axis)
+        got = lax.ppermute(sent, "dp", [(i, i ^ (1 << bit)) for i in range(count)])
+        total = kept.astype(jnp.float32) + got.astype(jnp.float32)
+        if bit != order[-1]:
+            total = total.astype(jnp.bfloat16)
+    return total.reshape(rows, terms.shape[1])
+
+
+def column_plan(width):
+    bits = lax.axis_size("dp").bit_length() - 1
+    plain = tuple(range(bits))
+    if bits < 3:
+        return [(0, width, plain)]
+    lanes = width // 128
+    first = lanes * 2 // 5 * 128
+    return [
+        (0, first, plain),
+        (first, 2 * first, (1, 0) + plain[2:]),
+        (2 * first, width, plain[2:] + (0, 1)),
+    ]
+
+
+def row_scatter(terms):
+    return jnp.concatenate(
+        [halving_sum(terms[:, lo:hi], order) for lo, hi, order in column_plan(terms.shape[1])],
+        axis=1,
+    )
+
+
+def grad_scatter(left, right):
+    parts = []
+    for lo, hi, order in column_plan(right.shape[1]):
+        terms = jnp.einsum(
+            "td,tf->df", left, right[:, lo:hi], preferred_element_type=jnp.float32
+        ).astype(jnp.bfloat16)
+        parts.append(halving_sum(terms, order))
+    return jnp.concatenate(parts, axis=1)
 
 
 def per_device(
@@ -67,33 +129,49 @@
     cotangent,
 ):
     half_rows = inputs.shape[0]
-    offset = lax.axis_index("tensor") * half_rows
-    (
-        query_weight,
-        key_weight,
-        value_weight,
-        output_weight,
-        gain_attn_in,
-        gain_attn_out,
-        gain_query,
-        gain_key,
-    ) = (
-        lax.all_gather(query_weight, "dp", axis=0, tiled=True),
-        lax.all_gather(key_weight, "dp", axis=0, tiled=True),
-        lax.all_gather(value_weight, "dp", axis=0, tiled=True),
-        lax.all_gather(output_weight, "dp", axis=0, tiled=True),
-        lax.all_gather(gain_attn_in, "dp", axis=0, tiled=True),
-        lax.all_gather(gain_attn_out, "dp", axis=0, tiled=True),
-        lax.all_gather(gain_query, "dp", axis=0, tiled=True),
-        lax.all_gather(gain_key, "dp", axis=0, tiled=True),
-    )
-    gate_weight, up_weight, down_weight, gain_ffn_in, gain_ffn_out = (
-        lax.all_gather(gate_weight, "dp", axis=0, tiled=True),
-        lax.all_gather(up_weight, "dp", axis=0, tiled=True),
-        lax.all_gather(down_weight, "dp", axis=0, tiled=True),
-        lax.all_gather(gain_ffn_in, "dp", axis=0, tiled=True),
-        lax.all_gather(gain_ffn_out, "dp", axis=0, tiled=True),
-    )
+    side = lax.axis_index("tensor")
+    count = lax.axis_size("dp")
+    offset = side * half_rows
+    head_dim = key_weight.shape[1]
+    width = query_weight.shape[1]
+    rows = query_weight.shape[0]
+    head_rows = gain_query.shape[0]
+    gain_columns = jnp.stack(
+        [
+            gain_attn_in,
+            gain_attn_out,
+            gain_ffn_in,
+            gain_ffn_out,
+            jnp.pad(gain_query, (0, rows - head_rows)),
+            jnp.pad(gain_key, (0, rows - head_rows)),
+        ],
+        axis=1,
+    )
+    packed = jnp.concatenate(
+        [
+            query_weight,
+            output_weight,
+            key_weight,
+            value_weight,
+            jnp.pad(gain_columns, ((0, 0), (0, 122))),
+        ],
+        axis=1,
+    )
+    packed = lax.all_gather(packed, "dp", axis=0, tiled=True)
+    query_weight = packed[:, :width]
+    output_weight = packed[:, width : 2 * width]
+    key_weight = packed[:, 2 * width : 2 * width + head_dim]
+    value_weight = packed[:, 2 * width + head_dim : 2 * width + 2 * head_dim]
+    gain_columns = packed[:, 2 * width + 2 * head_dim :]
+    gain_attn_in, gain_attn_out, gain_ffn_in, gain_ffn_out = (
+        gain_columns[:, i] for i in range(4)
+    )
+    gain_query, gain_key = (
+        gain_columns[:, i].reshape(count, rows)[:, :head_rows].reshape(-1) for i in (4, 5)
+    )
+    gate_weight = lax.all_gather(gate_weight, "dp", axis=0, tiled=True)
+    up_weight = lax.all_gather(up_weight, "dp", axis=0, tiled=True)
+    down_weight = lax.all_gather(down_weight, "dp", axis=0, tiled=True)
     gain_attn_in = gain_attn_in.astype(jnp.float32)
     gain_attn_out = gain_attn_out.astype(jnp.float32)
     gain_query = gain_query.astype(jnp.float32)
@@ -103,10 +181,20 @@
     residual_in = inputs.astype(jnp.float32)
     attn_normed_in, attn_hat, attn_inv = norm_rows(residual_in, gain_attn_in)
     attn_local = attn_normed_in.astype(jnp.bfloat16)
-    normed_rows = lax.all_gather(attn_local, "tensor", axis=0, tiled=True)
+    normed_rows = pair_rows(attn_local)
     seq_len = normed_rows.shape[0]
-    head_dim = key_weight.shape[1]
-    cosine, sine = rotary_tables(positions[0], head_dim)
+
+    def own_first(values):
+        return jnp.concatenate(
+            [
+                lax.dynamic_slice_in_dim(values, offset, half_rows, 0),
+                lax.dynamic_slice_in_dim(values, half_rows - offset, half_rows, 0),
+            ]
+        )
+
+    token_index = own_first(jnp.arange(seq_len))
+    documents = own_first(segments[0])
+    cosine, sine = rotary_tables(own_first(positions[0]), head_dim)
     query_raw = jnp.dot(normed_rows, query_weight, preferred_element_type=jnp.float32)
     local_heads = query_raw.shape[1] // head_dim
     query_raw = query_raw.reshape(seq_len, local_heads, head_dim)
@@ -120,9 +208,8 @@
     )
     key_normed, key_hat, key_inv = norm_rows(key_raw, gain_key)
     key_low = rotate(key_normed, cosine, sine).astype(jnp.bfloat16)
-    token_index = jnp.arange(seq_len)
     distance = token_index[:, None] - token_index[None, :]
-    allowed = (segments[0][:, None] == segments[0][None, :]) & (distance >= 0) & (distance < WINDOW)
+    allowed = (documents[:, None] == documents[None, :]) & (distance >= 0) & (distance < WINDOW)
     scores = jnp.einsum("thd,sd->hts", query_low, key_low, preferred_element_type=jnp.float32)
     scores = jnp.where(allowed[None], scores, NEG_FILL)
     row_max = jnp.max(scores, axis=-1, keepdims=True)
@@ -133,49 +220,41 @@
     context = jnp.einsum("hts,sd->thd", probs_low, value_low, preferred_element_type=jnp.float32)
     context = context.reshape(seq_len, local_heads * head_dim).astype(jnp.bfloat16)
     attn_terms = jnp.einsum("tc,dc->td", context, output_weight, preferred_element_type=jnp.float32)
-    attn_branch = lax.psum_scatter(attn_terms, "tensor", scatter_dimension=0, tiled=True)
+    attn_branch = pair_sum(attn_terms)
     post_attn, post_attn_hat, post_attn_inv = norm_rows(attn_branch, gain_attn_out)
     hidden_in = residual_in + post_attn
     ffn_normed, ffn_hat, ffn_inv = norm_rows(hidden_in, gain_ffn_in)
-    ffn_inputs = lax.all_gather(ffn_normed.astype(jnp.bfloat16), "tensor", axis=0, tiled=True)
+    ffn_inputs = pair_rows(ffn_normed.astype(jnp.bfloat16))
     gate_pre = jnp.dot(ffn_inputs, gate_weight, preferred_element_type=jnp.float32)
     upper_pre = jnp.dot(ffn_inputs, up_weight, preferred_element_type=jnp.float32)
     activated, gelu_pull = jax.vjp(gelu_product, gate_pre, upper_pre)
     hidden_low = activated.astype(jnp.bfloat16)
     ffn_terms = jnp.einsum("tf,df->td", hidden_low, down_weight, preferred_element_type=jnp.float32)
-    ffn_branch = lax.psum_scatter(ffn_terms, "tensor", scatter_dimension=0, tiled=True)
+    ffn_branch = pair_sum(ffn_terms)
     post_ffn, post_ffn_hat, post_ffn_inv = norm_rows(ffn_branch, gain_ffn_out)
     layer_out = (hidden_in + post_ffn).astype(jnp.bfloat16)
     out_grad = cotangent.astype(jnp.float32)
     ffn_branch_grad, gain_ffn_out_rows = norm_back(
         out_grad, post_ffn_hat, post_ffn_inv, gain_ffn_out
     )
-    ffn_grad_all = lax.all_gather(
-        ffn_branch_grad.astype(jnp.bfloat16), "tensor", axis=0, tiled=True
-    )
-    down_weight_grad = jnp.einsum(
-        "td,tf->df", ffn_grad_all, hidden_low, preferred_element_type=jnp.float32
-    )
+    ffn_grad_all = pair_rows(ffn_branch_grad.astype(jnp.bfloat16))
+    down_weight_grad = grad_scatter(ffn_grad_all, hidden_low)
     hidden_grad = jnp.dot(ffn_grad_all, down_weight, preferred_element_type=jnp.float32)
     gate_grad, upper_grad = gelu_pull(hidden_grad)
     gate_low = gate_grad.astype(jnp.bfloat16)
     upper_low = upper_grad.astype(jnp.bfloat16)
-    gate_weight_grad = jnp.einsum(
-        "td,tf->df", ffn_inputs, gate_low, preferred_element_type=jnp.float32
-    )
-    up_weight_grad = jnp.einsum(
-        "td,tf->df", ffn_inputs, upper_low, preferred_element_type=jnp.float32
-    )
+    gate_weight_grad = grad_scatter(ffn_inputs, gate_low)
+    up_weight_grad = grad_scatter(ffn_inputs, upper_low)
     ffn_in_terms = jnp.einsum(
         "tf,df->td", gate_low, gate_weight, preferred_element_type=jnp.float32
     ) + jnp.einsum("tf,df->td", upper_low, up_weight, preferred_element_type=jnp.float32)
-    ffn_in_grad = lax.psum_scatter(ffn_in_terms, "tensor", scatter_dimension=0, tiled=True)
+    ffn_in_grad = pair_sum(ffn_in_terms)
     ffn_norm_grad, gain_ffn_in_rows = norm_back(ffn_in_grad, ffn_hat, ffn_inv, gain_ffn_in)
     hidden_total = out_grad + ffn_norm_grad
     attn_branch_grad, gain_attn_out_rows = norm_back(
         hidden_total, post_attn_hat, post_attn_inv, gain_attn_out
     )
-    branch_all = lax.all_gather(attn_branch_grad.astype(jnp.bfloat16), "tensor", axis=0, tiled=True)
+    branch_all = pair_rows(attn_branch_grad.astype(jnp.bfloat16))
     output_weight_grad = jnp.einsum(
         "td,tc->dc", branch_all, context, preferred_element_type=jnp.float32
     )
@@ -207,21 +286,11 @@
     input_terms = jnp.einsum(
         "tc,dc->td", query_raw_low, query_weight, preferred_element_type=jnp.float32
     )
-    input_part, key_part, value_part = (
-        lax.psum_scatter(
-            input_terms.astype(jnp.bfloat16), "tensor", scatter_dimension=0, tiled=True
-        ).astype(jnp.float32),
-        lax.psum_scatter(
-            key_grad.astype(jnp.bfloat16), "tensor", scatter_dimension=0, tiled=True
-        ).astype(jnp.float32),
-        lax.psum_scatter(
-            value_grad.astype(jnp.bfloat16), "tensor", scatter_dimension=0, tiled=True
-        ).astype(jnp.float32),
-    )
-    local_cos = lax.dynamic_slice_in_dim(cosine, offset, half_rows, 0)
-    local_sin = lax.dynamic_slice_in_dim(sine, offset, half_rows, 0)
-    local_key_hat = lax.dynamic_slice_in_dim(key_hat, offset, half_rows, 0)
-    local_key_inv = lax.dynamic_slice_in_dim(key_inv, offset, half_rows, 0)
+    input_part = pair_sum(input_terms)
+    key_part = pair_sum(key_grad)
+    value_part = pair_sum(value_grad)
+    local_cos, local_sin = cosine[:half_rows], sine[:half_rows]
+    local_key_hat, local_key_inv = key_hat[:half_rows], key_inv[:half_rows]
     key_turned = rotate(key_part, local_cos, -local_sin)
     key_raw_grad, gain_key_rows = norm_back(key_turned, local_key_hat, local_key_inv, gain_key)
     key_raw_low = key_raw_grad.astype(jnp.bfloat16)
@@ -239,43 +308,52 @@
     )
     input_back, gain_attn_in_rows = norm_back(normed_grad, attn_hat, attn_inv, gain_attn_in)
     input_grad = hidden_total + input_back
-    query_weight_grad, output_weight_grad, gate_weight_grad, up_weight_grad, down_weight_grad = (
-        lax.psum_scatter(query_weight_grad, "dp", scatter_dimension=0, tiled=True),
-        lax.psum_scatter(output_weight_grad, "dp", scatter_dimension=0, tiled=True),
-        lax.psum_scatter(gate_weight_grad, "dp", scatter_dimension=0, tiled=True),
-        lax.psum_scatter(up_weight_grad, "dp", scatter_dimension=0, tiled=True),
-        lax.psum_scatter(down_weight_grad, "dp", scatter_dimension=0, tiled=True),
-    )
-    shared = (
-        lax.psum_scatter(key_weight_grad, ("dp", "tensor"), scatter_dimension=0, tiled=True),
-        lax.psum_scatter(value_weight_grad, ("dp", "tensor"), scatter_dimension=0, tiled=True),
-        lax.psum_scatter(
-            jnp.sum(gain_attn_in_rows, axis=0), ("dp", "tensor"), scatter_dimension=0, tiled=True
-        ),
-        lax.psum_scatter(
-            jnp.sum(gain_attn_out_rows, axis=0), ("dp", "tensor"), scatter_dimension=0, tiled=True
-        ),
-        lax.psum_scatter(gain_query_grad, ("dp", "tensor"), scatter_dimension=0, tiled=True),
-        lax.psum_scatter(
-            jnp.sum(gain_key_rows, axis=0), ("dp", "tensor"), scatter_dimension=0, tiled=True
-        ),
-        lax.psum_scatter(
-            jnp.sum(gain_ffn_in_rows, axis=0), ("dp", "tensor"), scatter_dimension=0, tiled=True
-        ),
-        lax.psum_scatter(
-            jnp.sum(gain_ffn_out_rows, axis=0), ("dp", "tensor"), scatter_dimension=0, tiled=True
-        ),
-    )
-    (
-        key_weight_grad,
-        value_weight_grad,
-        gain_attn_in_grad,
-        gain_attn_out_grad,
-        gain_query_grad,
-        gain_key_grad,
-        gain_ffn_in_grad,
-        gain_ffn_out_grad,
-    ) = shared
+    half_head_rows = head_rows // 2
+    half_weight_rows = rows // 2
+
+    def head_column(values):
+        blocks = values.reshape(count, 2, half_head_rows)
+        blocks = jnp.pad(blocks, ((0, 0), (0, 0), (0, half_weight_rows - half_head_rows)))
+        return blocks.reshape(-1)
+
+    gain_grads = jnp.stack(
+        [
+            jnp.sum(gain_attn_in_rows, axis=0),
+            jnp.sum(gain_attn_out_rows, axis=0),
+            jnp.sum(gain_ffn_in_rows, axis=0),
+            jnp.sum(gain_ffn_out_rows, axis=0),
+            head_column(gain_query_grad),
+            head_column(jnp.sum(gain_key_rows, axis=0)),
+        ],
+        axis=1,
+    )
+    summed = row_scatter(
+        jnp.concatenate(
+            [
+                query_weight_grad.astype(jnp.bfloat16),
+                output_weight_grad.astype(jnp.bfloat16),
+                key_weight_grad.astype(jnp.bfloat16),
+                value_weight_grad.astype(jnp.bfloat16),
+                jnp.pad(gain_grads, ((0, 0), (0, 122))).astype(jnp.bfloat16),
+            ],
+            axis=1,
+        )
+    )
+    query_weight_grad = summed[:, :width]
+    output_weight_grad = summed[:, width : 2 * width]
+    shared = summed[:, 2 * width :]
+    shared = lax.dynamic_slice_in_dim(
+        shared, side * half_weight_rows, half_weight_rows, 0
+    ) + swap_pair(
+        lax.dynamic_slice_in_dim(shared, (1 - side) * half_weight_rows, half_weight_rows, 0)
+    )
+    key_weight_grad = shared[:, :head_dim]
+    value_weight_grad = shared[:, head_dim : 2 * head_dim]
+    gain_grads = shared[:, 2 * head_dim :]
+    gain_attn_in_grad, gain_attn_out_grad, gain_ffn_in_grad, gain_ffn_out_grad = (
+        gain_grads[:, i] for i in range(4)
+    )
+    gain_query_grad, gain_key_grad = (gain_grads[:half_head_rows, i] for i in (4, 5))
     return (
         layer_out,
         input_grad,

time: 1840 us -> 932 us (0.51)
  waiting for transfers between devices: 1210 us -> 489 us
  blocking collectives: 297 us -> 0 us
  starting transfers between devices: 15.5 us -> 66.9 us
  local copies, waits for them, and re-layouts: 40.6 us -> 82.2 us
  other arithmetic: 46.3 us -> 66.7 us
    unnamed x31 -> x4, waiting for transfers between devices: 778 us -> 1.92 us
    unnamed x3 -> x0, blocking collectives: 212 us -> none
    ppermute x0 -> x59, waiting for transfers between devices: none -> 169 us  [the longest x48 161 us: halving_sum(): got = lax.ppermute(sent, 'dp', [(i, i ^ 1 << bit) for i in range(count)])]
    all_gather x2 -> x0, blocking collectives: 84.5 us -> none  [the longest x1 45.2 us: per_device(): lax.all_gather(value_weight, 'dp', axis=0, tiled=True)]
    reduce_scatter x8 -> x0, waiting for transfers between devices: 84.4 us -> none  [the longest x1 50.4 us: per_device(): lax.psum_scatter(query_weight_grad, 'dp', scatter_dimension=0, tiled=True)]
    ppermute x0 -> x59, starting transfers between devices: none -> 66.7 us  [the longest x48 64.6 us: halving_sum(): got = lax.ppermute(sent, 'dp', [(i, i ^ 1 << bit) for i in range(count)])]
    dynamic_slice x0 -> x52, local copies, waits for them, and re-layouts: none -> 25.7 us  [the longest x48 25.6 us: halving_sum(): sent = lax.dynamic_slice_in_dim(total, 1 - mine, 1, axis)]
    all_gather x9 -> x4, waiting for transfers between devices: 343 us -> 317 us  [the longest x1 94.8 us: per_device(): up_weight = lax.all_gather(up_weight, 'dp', axis=0, tiled=True)]
  transfers between devices with their start and end apart: 28 -> 63, of which waited for: 15 -> 31; matrix products, arithmetic and copies ran while one was open for 14% -> 33% of each run, Pallas kernels for 0% -> 0%
where the time goes in v1:
time: 932 us; the launch traced here: 921 us
  waiting for transfers between devices  489 us (52%)
  matrix products  200 us (21%)
  local copies, waits for them, and re-layouts  82.2 us (9%)
  starting transfers between devices  66.9 us (7%)
  other arithmetic  66.7 us (7%)
  between operations  16.4 us (2%)
    ppermute x48, waiting for transfers between devices, halving_sum(): got = lax.ppermute(sent, 'dp', [(i, i ^ 1 << bit) for i in range(count)])  161 us
    all_gather x1, waiting for transfers between devices, per_device(): up_weight = lax.all_gather(up_weight, 'dp', axis=0, tiled=True)  94.8 us
    all_gather x1, waiting for transfers between devices, per_device(): down_weight = lax.all_gather(down_weight, 'dp', axis=0, tiled=True)  89.8 us
    all_gather x1, waiting for transfers between devices, per_device(): packed = lax.all_gather(packed, 'dp', axis=0, tiled=True)  73.5 us
    ppermute x48, starting transfers between devices, halving_sum(): got = lax.ppermute(sent, 'dp', [(i, i ^ 1 << bit) for i in range(count)])  64.6 us
    all_gather x1, waiting for transfers between devices, per_device(): gate_weight = lax.all_gather(gate_weight, 'dp', axis=0, tiled=True)  59.3 us
    dot_general x9, matrix products, grad_scatter(): jnp.einsum('td,tf->df', left, right[:, lo:hi], preferred_element_type=jnp...  47 us
    dynamic_slice x48, local copies, waits for them, and re-layouts, halving_sum(): sent = lax.dynamic_slice_in_dim(total, 1 - mine, 1, axis)  25.6 us
  transfers between devices with their start and end apart: 63, of which 31 were waited for; matrix products, arithmetic and copies ran while one was open for 33% of the time, Pallas kernels for 0%

profile of v1, /device:TPU:0, one launch (start us, length us, event | category | flops | bytes accessed | tf_op | source)
XLA Modules:
  0.0 920.9 jit_solution(11072107506381844234)
XLA Ops:
  15.6 73.5 %all-gather.5.cloned.1.call-done = bf16[1152,1664]{1,0:T(8,128)(2,1)} async-done(((bf16[72,1664]{1,0:T(8,128)(2,1)}), bf16[1152,1664]{1,0:T(8,128)(2,1)}) %all-gather.5.cloned.1.call-update) | async-done | bytes 3833872 | tf_op jit(solution)/shard_map/all_gather | solution.py:160
  99.8 3.2 fusion.69
  107.1 4.5 multiply_reduce_fusion.8
  124.9 3.3 fusion.56
  140.1 59.3 %all-gather.7.cloned.1.call-done = bf16[1152,3456]{1,0:T(8,128)(2,1)} async-done(((bf16[72,3456]{1,0:T(8,128)(2,1)}), bf16[1152,3456]{1,0:T(8,128)(2,1)}) %all-gather.7.cloned.1.call-update) | async-done | bytes 7962640 | tf_op jit(solution)/shard_map/all_gather | solution.py:172
  199.4 15.2 %fusion.106 = f32[1024,3456]{1,0:T(8,128)} fusion(bf16[1152,3456]{1,0:T(8,128)(2,1)} %all-gather.7.cloned.1.call-done, bf16[512,1152]{1,0:T(8,128)(2,1)} %collective-permute-done.2, bf16[512,1152]{1,0:T(8,128)(2,1)S(1)} %multiply_convert_fusion.3), kind=kOutput, calls=%fused_computation.336 | convolution fusion | flops 8158445568 | bytes 24477696 | tf_op jit(solution)/shard_map/dot_general | solution.py:228
  214.5 94.8 %all-gather.9.cloned.1.call-done = bf16[1152,3456]{1,0:T(8,128)(2,1)} async-done(((bf16[72,3456]{1,0:T(8,128)(2,1)}), bf16[1152,3456]{1,0:T(8,128)(2,1)}) %all-gather.9.cloned.1.call-update) | async-done | bytes 7962640 | tf_op jit(solution)/shard_map/all_gather | solution.py:173
  309.3 19.9 %multiply_convert_fusion.1 = (bf16[1024,3456]{1,0:T(8,128)(2,1)}, f32[1024,3456]{1,0:T(8,128)}) fusion(f32[1024,3456]{1,0:T(8,128)} %fusion.106, bf16[1152,3456]{1,0:T(8,128)(2,1)} %all-gather.9.cloned.1.call-done, bf16[512,1152]{1,0:T(8,128)(2,1)} %collective-permute-done.2, bf16[512,1152]{1,0:T(8,128)(2,1)S(1)} %multiply_convert_fusion.3), kind=kOutput, calls=%fused_computation.10 | convolution fusion | flops 8193835008 | bytes 45711360 | tf_op jit(solution)/shard_map/dot_general | solution.py:229
  329.2 89.8 %all-gather.11.cloned.1.call-done = bf16[1152,3456]{1,0:T(8,128)(2,1)} async-done(((bf16[72,3456]{1,0:T(8,128)(2,1)}), bf16[1152,3456]{1,0:T(8,128)(2,1)}) %all-gather.11.cloned.1.call-update) | async-done | bytes 7962640 | tf_op jit(solution)/shard_map/all_gather | solution.py:174
  419.1 13.5 %fusion.108 = f32[1024,1152]{1,0:T(8,128)S(1)} fusion(bf16[1024,3456]{1,0:T(8,128)(2,1)} %get-tuple-element.79, bf16[1152,3456]{1,0:T(8,128)(2,1)} %all-gather.11.cloned.1.call-done), kind=kOutput, calls=%fused_computation.338 | convolution fusion | flops 8153726976 | bytes 19759104 | tf_op jit(solution)/shard_map/tf,df->td/dot_general | solution.py:232
  445.2 5.7 convolution_convert_fusion.1
  453.7 5.7 convolution_convert_fusion
  461.3 4.9 convolution_convert_fusion.6
  468.9 25.4 %multiply_convert_fusion = (bf16[1024,3456]{1,0:T(8,128)(2,1)}, bf16[1024,3456]{1,0:T(8,128)(2,1)}) fusion(f32[1024,3456]{1,0:T(8,128)} %fusion.106, f32[1024,3456]{1,0:T(8,128)} %get-tuple-element.80, bf16[1152,3456]{1,0:T(8,128)(2,1)} %all-gather.11.cloned.1.call-done, bf16[512,1152]{1,0:T(8,128)(2,1)} %collective-permute-done.4, ...), kind=kOutput, calls=%fused_computation.9 | convolution fusion | flops 8243380224 | bytes 52789248 | tf_op jit(solution)/shard_map/dot_general | solution.py:242
  494.3 5.5 convolution_convert_fusion.3
  502.7 4.6 convolution_convert_fusion.2
  508.5 5.4 convolution_convert_fusion.7
  516.7 3.9 convolution_convert_fusion.8
  523.5 6.7 convolution_convert_fusion.5
  530.3 4.6 convolution_convert_fusion.4
  534.9 14.5 %fusion.109 = f32[1024,1152]{1,0:T(8,128)} fusion(bf16[1024,3456]{1,0:T(8,128)(2,1)S(1)} %bitcast.192, bf16[1152,3456]{1,0:T(8,128)(2,1)} %all-gather.7.cloned.1.call-done), kind=kOutput, calls=%fused_computation.339 | convolution fusion | flops 8153726976 | bytes 19759104 | tf_op jit(solution)/shard_map/tf,df->td/dot_general | solution.py:248
  549.4 14.9 %convolution_add_fusion = f32[1024,1152]{1,0:T(8,128)S(1)} fusion(f32[1024,1152]{1,0:T(8,128)} %fusion.109, bf16[1024,3456]{1,0:T(8,128)(2,1)} %get-tuple-element.42, bf16[1152,3456]{1,0:T(8,128)(2,1)} %all-gather.9.cloned.1.call-done), kind=kOutput, calls=%fused_computation.32 | convolution fusion | flops 8154906624 | bytes 24477696 | tf_op jit(solution)/shard_map/tf,df->td/dot_general | solution.py:250
  584.6 18.7 %collective-permute-done.35 = bf16[2,2,2,1,72,1280]{5,4,3,2,1,0:T(8,128)(2,1)S(1)} collective-permute-done((bf16[2,2,2,1,72,1280]{5,4,3,2,1,0:T(8,128)(2,1)S(1)}, bf16[2,2,2,1,72,1280]{5,4,3,2,1,0:T(8,128)(2,1)S(1)}, u32[]{:S(2)}, u32[]{:S(2)}) %collective-permute-start.35) | collective-permute-done | bytes 1474592 | tf_op jit(solution)/shard_map/ppermute | solution.py:74
  611.3 23.0 %collective-permute-done.23 = bf16[2,2,2,1,72,1280]{5,4,3,2,1,0:T(8,128)(2,1)S(1)} collective-permute-done((bf16[2,2,2,1,72,1280]{5,4,3,2,1,0:T(8,128)(2,1)S(1)}, bf16[2,2,2,1,72,1280]{5,4,3,2,1,0:T(8,128)(2,1)S(1)}, u32[]{:S(2)}, u32[]{:S(2)}) %collective-permute-start.23) | collective-permute-done | bytes 1474592 | tf_op jit(solution)/shard_map/ppermute | solution.py:74
  638.5 12.7 %collective-permute-done.56 = bf16[1,1,2,2,72,896]{5,4,3,2,1,0:T(8,128)(2,1)S(1)} collective-permute-done((bf16[1,1,2,2,72,896]{5,4,3,2,1,0:T(8,128)(2,1)S(1)}, bf16[1,1,2,2,72,896]{5,4,3,2,1,0:T(8,128)(2,1)S(1)}, u32[]{:S(2)}, u32[]{:S(2)}) %collective-permute-start.56) | collective-permute-done | bytes 516128 | tf_op jit(solution)/shard_map/ppermute | solution.py:74
  652.8 9.4 %collective-permute-done.44 = bf16[1,1,2,2,72,896]{5,4,3,2,1,0:T(8,128)(2,1)S(1)} collective-permute-done((bf16[1,1,2,2,72,896]{5,4,3,2,1,0:T(8,128)(2,1)S(1)}, bf16[1,1,2,2,72,896]{5,4,3,2,1,0:T(8,128)(2,1)S(1)}, u32[]{:S(2)}, u32[]{:S(2)}) %collective-permute-start.44) | collective-permute-done | bytes 516128 | tf_op jit(solution)/shard_map/ppermute | solution.py:74
  663.9 8.2 collective-permute-done.32
  674.5 6.8 collective-permute-done.45
  686.3 13.5 %collective-permute-done.58 = bf16[1,1,1,1,72,896]{5,4,3,2,1,0:T(8,128)(2,1)S(1)} collective-permute-done((bf16[1,1,1,1,72,896]{5,4,3,2,1,0:T(8,128)(2,1)S(1)}, bf16[1,1,1,1,72,896]{5,4,3,2,1,0:T(8,128)(2,1)S(1)}, u32[]{:S(2)}, u32[]{:S(2)}) %collective-permute-start.58) | collective-permute-done | bytes 129056 | tf_op jit(solution)/shard_map/ppermute | solution.py:74
  706.9 4.1 collective-permute-done.34
  720.0 9.0 collective-permute-done.40
  733.5 3.3 collective-permute-done.28
  736.9 3.8 collective-permute-start.41
  742.0 4.0 fusion.55
  767.6 3.3 fusion.64
  779.1 3.2 convolution_convert_fusion.10
  791.6 3.4 collective-permute-start.50
  812.1 3.8 copy.108
  823.4 8.9 collective-permute-done.38
  840.1 3.5 collective-permute-done.30
  844.7 5.3 collective-permute-done.14
  858.3 4.8 fusion.41
  871.0 3.8 fusion.40
  879.3 6.8 collective-permute-done.16
  886.2 4.1 collective-permute-start.17
  893.6 7.8 collective-permute-done.19
  902.3 4.0 collective-permute-done.20
  907.2 3.5 collective-permute-done.21
  (594 shorter events, 243.0 us)
Async XLA Ops:
  7.2 81.9 %all-gather.5.cloned.1.call-start = ((), (), s32[]{:S(2)}) async-start(), calls=%async_computation | async-start | bytes 4073472 | tf_op jit(solution)/shard_map/all_gather | solution.py:160
  12.9 186.5 %all-gather.7.cloned.1.call-start = ((), (), s32[]{:S(2)}) async-start(), calls=%async_computation.1 | async-start | bytes 8460288 | tf_op jit(solution)/shard_map/all_gather | solution.py:172
  13.7 295.6 %all-gather.9.cloned.1.call-start = ((), (), s32[]{:S(2)}) async-start(), calls=%async_computation.2 | async-start | bytes 8460288 | tf_op jit(solution)/shard_map/all_gather | solution.py:173
  14.4 404.7 %all-gather.11.cloned.1.call-start = ((), (), s32[]{:S(2)}) async-start(), calls=%async_computation.3 | async-start | bytes 8460288 | tf_op jit(solution)/shard_map/all_gather | solution.py:174
  452.2 129.3 %collective-permute-start.47 = (bf16[2,2,2,1,72,1280]{5,4,3,2,1,0:T(8,128)(2,1)}, bf16[2,2,2,1,72,1280]{5,4,3,2,1,0:T(8,128)(2,1)}, u32[]{:S(2)}, u32[]{:S(2)}) collective-permute-start(bf16[2,2,2,1,72,1280]{5,4,3,2,1,0:T(8,128)(2,1)} %constant_dynamic-slice_fusion.11), channel_id=1, source_target_pairs={{0,2},{2,0},{4,6},{6,4},{8,10},{10,8},{12,14},{14,12},{16,18},{18,... | collective-permute-start | bytes 4423688 | tf_op jit(solution)/shard_map/ppermute | solution.py:74
  460.7 144.5 %collective-permute-start.51 = (bf16[2,2,1,2,72,1280]{5,4,3,2,1,0:T(8,128)(2,1)}, bf16[2,2,1,2,72,1280]{5,4,3,2,1,0:T(8,128)(2,1)}, u32[]{:S(2)}, u32[]{:S(2)}) collective-permute-start(bf16[2,2,1,2,72,1280]{5,4,3,2,1,0:T(8,128)(2,1)} %constant_dynamic-slice_fusion.7), channel_id=1, source_target_pairs={{0,4},{2,6},{4,0},{6,2},{8,12},{10,14},{12,8},{14,10},{16,20},{18,... | collective-permute-start | bytes 4423688 | tf_op jit(solution)/shard_map/ppermute | solution.py:74
  468.5 97.7 %collective-permute-start.55 = (bf16[2,1,2,2,72,896]{5,4,3,2,1,0:T(8,128)(2,1)}, bf16[2,1,2,2,72,896]{5,4,3,2,1,0:T(8,128)(2,1)}, u32[]{:S(2)}, u32[]{:S(2)}) collective-permute-start(bf16[2,1,2,2,72,896]{5,4,3,2,1,0:T(8,128)(2,1)} %constant_dynamic-slice_fusion.3), channel_id=1, source_target_pairs={{0,8},{2,10},{4,12},{6,14},{8,0},{10,2},{12,4},{14,6},{16,24},{18,... | collective-permute-start | bytes 3096584 | tf_op jit(solution)/shard_map/ppermute | solution.py:74
  515.1 53.0 %collective-permute-start.43 = (bf16[2,1,2,2,72,896]{5,4,3,2,1,0:T(8,128)(2,1)}, bf16[2,1,2,2,72,896]{5,4,3,2,1,0:T(8,128)(2,1)}, u32[]{:S(2)}, u32[]{:S(2)}) collective-permute-start(bf16[2,1,2,2,72,896]{5,4,3,2,1,0:T(8,128)(2,1)} %constant_dynamic-slice_fusion.15), channel_id=1, source_target_pairs={{0,8},{2,10},{4,12},{6,14},{8,0},{10,2},{12,4},{14,6},{16,24},{18,... | collective-permute-start | bytes 3096584 | tf_op jit(solution)/shard_map/ppermute | solution.py:74
  523.1 48.2 %collective-permute-start.31 = (bf16[2,1,2,2,72,896]{5,4,3,2,1,0:T(8,128)(2,1)}, bf16[2,1,2,2,72,896]{5,4,3,2,1,0:T(8,128)(2,1)}, u32[]{:S(2)}, u32[]{:S(2)}) collective-permute-start(bf16[2,1,2,2,72,896]{5,4,3,2,1,0:T(8,128)(2,1)} %constant_dynamic-slice_fusion.27), channel_id=1, source_target_pairs={{0,8},{2,10},{4,12},{6,14},{8,0},{10,2},{12,4},{14,6},{16,24},{18,... | collective-permute-start | bytes 3096584 | tf_op jit(solution)/shard_map/ppermute | solution.py:74
  568.1 35.2 %collective-permute-start.35 = (bf16[2,2,2,1,72,1280]{5,4,3,2,1,0:T(8,128)(2,1)S(1)}, bf16[2,2,2,1,72,1280]{5,4,3,2,1,0:T(8,128)(2,1)S(1)}, u32[]{:S(2)}, u32[]{:S(2)}) collective-permute-start(bf16[2,2,2,1,72,1280]{5,4,3,2,1,0:T(8,128)(2,1)S(1)} %copy-done.61), channel_id=1, source_target_pairs={{0,2},{2,0},{4,6},{6,4},{8,10},{10,8},{12,14},{14,12},{16,18},{18,... | collective-permute-start | bytes 4423688 | tf_op jit(solution)/shard_map/ppermute | solution.py:74
  571.3 37.3 %collective-permute-start.39 = (bf16[2,2,1,2,72,1280]{5,4,3,2,1,0:T(8,128)(2,1)S(1)}, bf16[2,2,1,2,72,1280]{5,4,3,2,1,0:T(8,128)(2,1)S(1)}, u32[]{:S(2)}, u32[]{:S(2)}) collective-permute-start(bf16[2,2,1,2,72,1280]{5,4,3,2,1,0:T(8,128)(2,1)S(1)} %copy-done.60), channel_id=1, source_target_pairs={{0,4},{2,6},{4,0},{6,2},{8,12},{10,14},{12,8},{14,10},{16,20},{18,... | collective-permute-start | bytes 4423688 | tf_op jit(solution)/shard_map/ppermute | solution.py:74
  574.9 59.4 %collective-permute-start.23 = (bf16[2,2,2,1,72,1280]{5,4,3,2,1,0:T(8,128)(2,1)S(1)}, bf16[2,2,2,1,72,1280]{5,4,3,2,1,0:T(8,128)(2,1)S(1)}, u32[]{:S(2)}, u32[]{:S(2)}) collective-permute-start(bf16[2,2,2,1,72,1280]{5,4,3,2,1,0:T(8,128)(2,1)S(1)} %constant_dynamic-slice_fusion.35), channel_id=1, source_target_pairs={{0,2},{2,0},{4,6},{6,4},{8,10},{10,8},{12,14},{14,12},{16,18},{18,... | collective-permute-start | bytes 4423688 | tf_op jit(solution)/shard_map/ppermute | solution.py:74
  581.6 55.6 %collective-permute-start.27 = (bf16[2,2,1,2,72,1280]{5,4,3,2,1,0:T(8,128)(2,1)S(1)}, bf16[2,2,1,2,72,1280]{5,4,3,2,1,0:T(8,128)(2,1)S(1)}, u32[]{:S(2)}, u32[]{:S(2)}) collective-permute-start(bf16[2,2,1,2,72,1280]{5,4,3,2,1,0:T(8,128)(2,1)S(1)} %constant_dynamic-slice_fusion.31), channel_id=1, source_target_pairs={{0,4},{2,6},{4,0},{6,2},{8,12},{10,14},{12,8},{14,10},{16,20},{18,... | collective-permute-start | bytes 4423688 | tf_op jit(solution)/shard_map/ppermute | solution.py:74
  603.3 47.9 %collective-permute-start.56 = (bf16[1,1,2,2,72,896]{5,4,3,2,1,0:T(8,128)(2,1)S(1)}, bf16[1,1,2,2,72,896]{5,4,3,2,1,0:T(8,128)(2,1)S(1)}, u32[]{:S(2)}, u32[]{:S(2)}) collective-permute-start(bf16[1,1,2,2,72,896]{5,4,3,2,1,0:T(8,128)(2,1)S(1)} %constant_dynamic-slice_fusion.2), channel_id=1, source_target_pairs={{0,16},{2,18},{4,20},{6,22},{8,24},{10,26},{12,28},{14,30},{16,0},... | collective-permute-start | bytes 1548296 | tf_op jit(solution)/shard_map/ppermute | solution.py:74
  605.2 57.0 %collective-permute-start.44 = (bf16[1,1,2,2,72,896]{5,4,3,2,1,0:T(8,128)(2,1)S(1)}, bf16[1,1,2,2,72,896]{5,4,3,2,1,0:T(8,128)(2,1)S(1)}, u32[]{:S(2)}, u32[]{:S(2)}) collective-permute-start(bf16[1,1,2,2,72,896]{5,4,3,2,1,0:T(8,128)(2,1)S(1)} %constant_dynamic-slice_fusion.14), channel_id=1, source_target_pairs={{0,16},{2,18},{4,20},{6,22},{8,24},{10,26},{12,28},{14,30},{16,0},... | collective-permute-start | bytes 1548296 | tf_op jit(solution)/shard_map/ppermute | solution.py:74
  609.4 62.7 %collective-permute-start.32 = (bf16[1,1,2,2,72,896]{5,4,3,2,1,0:T(8,128)(2,1)S(1)}, bf16[1,1,2,2,72,896]{5,4,3,2,1,0:T(8,128)(2,1)S(1)}, u32[]{:S(2)}, u32[]{:S(2)}) collective-permute-start(bf16[1,1,2,2,72,896]{5,4,3,2,1,0:T(8,128)(2,1)S(1)} %copy-done.90), channel_id=1, source_target_pairs={{0,16},{2,18},{4,20},{6,22},{8,24},{10,26},{12,28},{14,30},{16,0},... | collective-permute-start | bytes 1548296 | tf_op jit(solution)/shard_map/ppermute | solution.py:74
  634.3 107.6 %collective-permute-start.6 = (bf16[512,1152]{1,0:T(8,128)(2,1)S(1)}, bf16[512,1152]{1,0:T(8,128)(2,1)S(1)}, u32[]{:S(2)}, u32[]{:S(2)}) collective-permute-start(bf16[512,1152]{1,0:T(8,128)(2,1)S(1)} %multiply_convert_fusion.2), channel_id=1, source_target_pairs={{0,1},{1,0},{2,3},{3,2},{4,5},{5,4},{6,7},{7,6},{8,9},{9,8},{10,11... | collective-permute-start | bytes 3538952 | tf_op jit(solution)/shard_map/ppermute | solution.py:51
  637.2 76.1 %collective-permute-start.48 = (bf16[2,2,1,1,72,1280]{5,4,3,2,1,0:T(8,128)(2,1)S(1)}, bf16[2,2,1,1,72,1280]{5,4,3,2,1,0:T(8,128)(2,1)S(1)}, u32[]{:S(2)}, u32[]{:S(2)}) collective-permute-start(bf16[2,2,1,1,72,1280]{5,4,3,2,1,0:T(8,128)(2,1)S(1)} %constant_dynamic-slice_fusion.10), channel_id=1, source_target_pairs={{0,4},{2,6},{4,0},{6,2},{8,12},{10,14},{12,8},{14,10},{16,20},{18,... | collective-permute-start | bytes 2211848 | tf_op jit(solution)/shard_map/ppermute | solution.py:74
  651.2 63.6 %collective-permute-start.52 = (bf16[2,2,1,1,72,1280]{5,4,3,2,1,0:T(8,128)(2,1)S(1)}, bf16[2,2,1,1,72,1280]{5,4,3,2,1,0:T(8,128)(2,1)S(1)}, u32[]{:S(2)}, u32[]{:S(2)}) collective-permute-start(bf16[2,2,1,1,72,1280]{5,4,3,2,1,0:T(8,128)(2,1)S(1)} %constant_dynamic-slice_fusion.6), channel_id=1, source_target_pairs={{0,2},{2,0},{4,6},{6,4},{8,10},{10,8},{12,14},{14,12},{16,18},{18,... | collective-permute-start | bytes 2211848 | tf_op jit(solution)/shard_map/ppermute | solution.py:74
  662.2 11.5 %collective-permute-start.57 = (bf16[1,1,2,1,72,896]{5,4,3,2,1,0:T(8,128)(2,1)S(1)}, bf16[1,1,2,1,72,896]{5,4,3,2,1,0:T(8,128)(2,1)S(1)}, u32[]{:S(2)}, u32[]{:S(2)}) collective-permute-start(bf16[1,1,2,1,72,896]{5,4,3,2,1,0:T(8,128)(2,1)S(1)} %constant_dynamic-slice_fusion.1), channel_id=1, source_target_pairs={{0,2},{2,0},{4,6},{6,4},{8,10},{10,8},{12,14},{14,12},{16,18},{18,... | collective-permute-start | bytes 774152 | tf_op jit(solution)/shard_map/ppermute | solution.py:74
  673.8 10.9 %collective-permute-start.33 = (bf16[1,1,2,1,72,896]{5,4,3,2,1,0:T(8,128)(2,1)S(1)}, bf16[1,1,2,1,72,896]{5,4,3,2,1,0:T(8,128)(2,1)S(1)}, u32[]{:S(2)}, u32[]{:S(2)}) collective-permute-start(bf16[1,1,2,1,72,896]{5,4,3,2,1,0:T(8,128)(2,1)S(1)} %constant_dynamic-slice_fusion.25), channel_id=1, source_target_pairs={{0,2},{2,0},{4,6},{6,4},{8,10},{10,8},{12,14},{14,12},{16,18},{18,... | collective-permute-start | bytes 774152 | tf_op jit(solution)/shard_map/ppermute | solution.py:74
  681.3 36.1 %collective-permute-start.36 = (bf16[2,2,1,1,72,1280]{5,4,3,2,1,0:T(8,128)(2,1)S(1)}, bf16[2,2,1,1,72,1280]{5,4,3,2,1,0:T(8,128)(2,1)S(1)}, u32[]{:S(2)}, u32[]{:S(2)}) collective-permute-start(bf16[2,2,1,1,72,1280]{5,4,3,2,1,0:T(8,128)(2,1)S(1)} %constant_dynamic-slice_fusion.22), channel_id=1, source_target_pairs={{0,4},{2,6},{4,0},{6,2},{8,12},{10,14},{12,8},{14,10},{16,20},{18,... | collective-permute-start | bytes 2211848 | tf_op jit(solution)/shard_map/ppermute | solution.py:74
  684.7 15.0 %collective-permute-start.58 = (bf16[1,1,1,1,72,896]{5,4,3,2,1,0:T(8,128)(2,1)S(1)}, bf16[1,1,1,1,72,896]{5,4,3,2,1,0:T(8,128)(2,1)S(1)}, u32[]{:S(2)}, u32[]{:S(2)}) collective-permute-start(bf16[1,1,1,1,72,896]{5,4,3,2,1,0:T(8,128)(2,1)S(1)} %constant_dynamic-slice_fusion), channel_id=1, source_target_pairs={{0,4},{2,6},{4,0},{6,2},{8,12},{10,14},{12,8},{14,10},{16,20},{18,... | collective-permute-start | bytes 387080 | tf_op jit(solution)/shard_map/ppermute | solution.py:74
  711.0 18.0 %collective-permute-start.40 = (bf16[2,2,1,1,72,1280]{5,4,3,2,1,0:T(8,128)(2,1)S(1)}, bf16[2,2,1,1,72,1280]{5,4,3,2,1,0:T(8,128)(2,1)S(1)}, u32[]{:S(2)}, u32[]{:S(2)}) collective-permute-start(bf16[2,2,1,1,72,1280]{5,4,3,2,1,0:T(8,128)(2,1)S(1)} %constant_dynamic-slice_fusion.18), channel_id=1, source_target_pairs={{0,2},{2,0},{4,6},{6,4},{8,10},{10,8},{12,14},{14,12},{16,18},{18,... | collective-permute-start | bytes 2211848 | tf_op jit(solution)/shard_map/ppermute | solution.py:74
  713.2 18.4 %collective-permute-start.24 = (bf16[2,2,1,1,72,1280]{5,4,3,2,1,0:T(8,128)(2,1)S(1)}, bf16[2,2,1,1,72,1280]{5,4,3,2,1,0:T(8,128)(2,1)S(1)}, u32[]{:S(2)}, u32[]{:S(2)}) collective-permute-start(bf16[2,2,1,1,72,1280]{5,4,3,2,1,0:T(8,128)(2,1)S(1)} %constant_dynamic-slice_fusion.34), channel_id=1, source_target_pairs={{0,4},{2,6},{4,0},{6,2},{8,12},{10,14},{12,8},{14,10},{16,20},{18,... | collective-permute-start | bytes 2211848 | tf_op jit(solution)/shard_map/ppermute | solution.py:74
  714.8 22.1 %collective-permute-start.28 = (bf16[2,2,1,1,72,1280]{5,4,3,2,1,0:T(8,128)(2,1)S(1)}, bf16[2,2,1,1,72,1280]{5,4,3,2,1,0:T(8,128)(2,1)S(1)}, u32[]{:S(2)}, u32[]{:S(2)}) collective-permute-start(bf16[2,2,1,1,72,1280]{5,4,3,2,1,0:T(8,128)(2,1)S(1)} %constant_dynamic-slice_fusion.30), channel_id=1, source_target_pairs={{0,2},{2,0},{4,6},{6,4},{8,10},{10,8},{12,14},{14,12},{16,18},{18,... | collective-permute-start | bytes 2211848 | tf_op jit(solution)/shard_map/ppermute | solution.py:74
  717.5 64.9 %collective-permute-start.49 = (bf16[2,1,1,1,72,1280]{5,4,3,2,1,0:T(8,128)(2,1)}, bf16[2,1,1,1,72,1280]{5,4,3,2,1,0:T(8,128)(2,1)}, u32[]{:S(2)}, u32[]{:S(2)}) collective-permute-start(bf16[2,1,1,1,72,1280]{5,4,3,2,1,0:T(8,128)(2,1)} %constant_dynamic-slice_fusion.9), channel_id=1, source_target_pairs={{0,8},{2,10},{4,12},{6,14},{8,0},{10,2},{12,4},{14,6},{16,24},{18,... | collective-permute-start | bytes 1105928 | tf_op jit(solution)/shard_map/ppermute | solution.py:74
  729.0 55.5 %collective-permute-start.53 = (bf16[2,1,1,1,72,1280]{5,4,3,2,1,0:T(8,128)(2,1)}, bf16[2,1,1,1,72,1280]{5,4,3,2,1,0:T(8,128)(2,1)}, u32[]{:S(2)}, u32[]{:S(2)}) collective-permute-start(bf16[2,1,1,1,72,1280]{5,4,3,2,1,0:T(8,128)(2,1)} %constant_dynamic-slice_fusion.5), channel_id=1, source_target_pairs={{0,8},{2,10},{4,12},{6,14},{8,0},{10,2},{12,4},{14,6},{16,24},{18,... | collective-permute-start | bytes 1105928 | tf_op jit(solution)/shard_map/ppermute | solution.py:74
  731.6 55.6 %collective-permute-start.37 = (bf16[2,1,1,1,72,1280]{5,4,3,2,1,0:T(8,128)(2,1)}, bf16[2,1,1,1,72,1280]{5,4,3,2,1,0:T(8,128)(2,1)}, u32[]{:S(2)}, u32[]{:S(2)}) collective-permute-start(bf16[2,1,1,1,72,1280]{5,4,3,2,1,0:T(8,128)(2,1)} %constant_dynamic-slice_fusion.21), channel_id=1, source_target_pairs={{0,8},{2,10},{4,12},{6,14},{8,0},{10,2},{12,4},{14,6},{16,24},{18,... | collective-permute-start | bytes 1105928 | tf_op jit(solution)/shard_map/ppermute | solution.py:74
  736.9 51.7 %collective-permute-start.41 = (bf16[2,1,1,1,72,1280]{5,4,3,2,1,0:T(8,128)(2,1)}, bf16[2,1,1,1,72,1280]{5,4,3,2,1,0:T(8,128)(2,1)}, u32[]{:S(2)}, u32[]{:S(2)}) collective-permute-start(bf16[2,1,1,1,72,1280]{5,4,3,2,1,0:T(8,128)(2,1)} %constant_dynamic-slice_fusion.17), channel_id=1, source_target_pairs={{0,8},{2,10},{4,12},{6,14},{8,0},{10,2},{12,4},{14,6},{16,24},{18,... | collective-permute-start | bytes 1105928 | tf_op jit(solution)/shard_map/ppermute | solution.py:74
  741.9 49.7 %collective-permute-start.25 = (bf16[2,1,1,1,72,1280]{5,4,3,2,1,0:T(8,128)(2,1)}, bf16[2,1,1,1,72,1280]{5,4,3,2,1,0:T(8,128)(2,1)}, u32[]{:S(2)}, u32[]{:S(2)}) collective-permute-start(bf16[2,1,1,1,72,1280]{5,4,3,2,1,0:T(8,128)(2,1)} %constant_dynamic-slice_fusion.33), channel_id=1, source_target_pairs={{0,8},{2,10},{4,12},{6,14},{8,0},{10,2},{12,4},{14,6},{16,24},{18,... | collective-permute-start | bytes 1105928 | tf_op jit(solution)/shard_map/ppermute | solution.py:74
  782.4 13.6 %collective-permute-start.29 = (bf16[2,1,1,1,72,1280]{5,4,3,2,1,0:T(8,128)(2,1)S(1)}, bf16[2,1,1,1,72,1280]{5,4,3,2,1,0:T(8,128)(2,1)S(1)}, u32[]{:S(2)}, u32[]{:S(2)}) collective-permute-start(bf16[2,1,1,1,72,1280]{5,4,3,2,1,0:T(8,128)(2,1)S(1)} %copy-done.92), channel_id=1, source_target_pairs={{0,8},{2,10},{4,12},{6,14},{8,0},{10,2},{12,4},{14,6},{16,24},{18,... | collective-permute-start | bytes 1105928 | tf_op jit(solution)/shard_map/ppermute | solution.py:74
  784.5 23.4 %collective-permute-start.9 = (bf16[512,256]{1,0:T(8,128)(2,1)}, bf16[512,256]{1,0:T(8,128)(2,1)}, u32[]{:S(2)}, u32[]{:S(2)}) collective-permute-start(bf16[512,256]{1,0:T(8,128)(2,1)} %slice.438), channel_id=1, source_target_pairs={{0,1},{1,0},{2,3},{3,2},{4,5},{5,4},{6,7},{7,6},{8,9},{9,8},{10,11... | collective-permute-start | bytes 786440 | tf_op jit(solution)/shard_map/ppermute | solution.py:51
  787.2 71.0 %collective-permute-start.7 = (bf16[512,1152]{1,0:T(8,128)(2,1)}, bf16[512,1152]{1,0:T(8,128)(2,1)}, u32[]{:S(2)}, u32[]{:S(2)}) collective-permute-start(bf16[512,1152]{1,0:T(8,128)(2,1)} %slice.434), channel_id=1, source_target_pairs={{0,1},{1,0},{2,3},{3,2},{4,5},{5,4},{6,7},{7,6},{8,9},{9,8},{10,11... | collective-permute-start | bytes 3538952 | tf_op jit(solution)/shard_map/ppermute | solution.py:51
  791.6 25.7 %collective-permute-start.50 = (bf16[1,1,1,1,72,1280]{5,4,3,2,1,0:T(8,128)(2,1)}, bf16[1,1,1,1,72,1280]{5,4,3,2,1,0:T(8,128)(2,1)}, u32[]{:S(2)}, u32[]{:S(2)}) collective-permute-start(bf16[1,1,1,1,72,1280]{5,4,3,2,1,0:T(8,128)(2,1)} %constant_dynamic-slice_fusion.8), channel_id=1, source_target_pairs={{0,16},{2,18},{4,20},{6,22},{8,24},{10,26},{12,28},{14,30},{16,0},... | collective-permute-start | bytes 552968 | tf_op jit(solution)/shard_map/ppermute | solution.py:74
  796.1 25.1 %collective-permute-start.54 = (bf16[1,1,1,1,72,1280]{5,4,3,2,1,0:T(8,128)(2,1)}, bf16[1,1,1,1,72,1280]{5,4,3,2,1,0:T(8,128)(2,1)}, u32[]{:S(2)}, u32[]{:S(2)}) collective-permute-start(bf16[1,1,1,1,72,1280]{5,4,3,2,1,0:T(8,128)(2,1)} %constant_dynamic-slice_fusion.4), channel_id=1, source_target_pairs={{0,16},{2,18},{4,20},{6,22},{8,24},{10,26},{12,28},{14,30},{16,0},... | collective-permute-start | bytes 552968 | tf_op jit(solution)/shard_map/ppermute | solution.py:74
  797.7 34.6 %collective-permute-start.38 = (bf16[1,1,1,1,72,1280]{5,4,3,2,1,0:T(8,128)(2,1)}, bf16[1,1,1,1,72,1280]{5,4,3,2,1,0:T(8,128)(2,1)}, u32[]{:S(2)}, u32[]{:S(2)}) collective-permute-start(bf16[1,1,1,1,72,1280]{5,4,3,2,1,0:T(8,128)(2,1)} %constant_dynamic-slice_fusion.20), channel_id=1, source_target_pairs={{0,16},{2,18},{4,20},{6,22},{8,24},{10,26},{12,28},{14,30},{16,0},... | collective-permute-start | bytes 552968 | tf_op jit(solution)/shard_map/ppermute | solution.py:74
  807.9 28.3 %collective-permute-start.42 = (bf16[1,1,1,1,72,1280]{5,4,3,2,1,0:T(8,128)(2,1)}, bf16[1,1,1,1,72,1280]{5,4,3,2,1,0:T(8,128)(2,1)}, u32[]{:S(2)}, u32[]{:S(2)}) collective-permute-start(bf16[1,1,1,1,72,1280]{5,4,3,2,1,0:T(8,128)(2,1)} %constant_dynamic-slice_fusion.16), channel_id=1, source_target_pairs={{0,16},{2,18},{4,20},{6,22},{8,24},{10,26},{12,28},{14,30},{16,0},... | collective-permute-start | bytes 552968 | tf_op jit(solution)/shard_map/ppermute | solution.py:74
  817.2 22.8 %collective-permute-start.26 = (bf16[1,1,1,1,72,1280]{5,4,3,2,1,0:T(8,128)(2,1)}, bf16[1,1,1,1,72,1280]{5,4,3,2,1,0:T(8,128)(2,1)S(1)}, u32[]{:S(2)}, u32[]{:S(2)}) collective-permute-start(bf16[1,1,1,1,72,1280]{5,4,3,2,1,0:T(8,128)(2,1)} %constant_dynamic-slice_fusion.32), channel_id=1, source_target_pairs={{0,16},{2,18},{4,20},{6,22},{8,24},{10,26},{12,28},{14,30},{16,0},... | collective-permute-start | bytes 552968 | tf_op jit(solution)/shard_map/ppermute | solution.py:74
  821.2 22.5 %collective-permute-start.30 = (bf16[1,1,1,1,72,1280]{5,4,3,2,1,0:T(8,128)(2,1)}, bf16[1,1,1,1,72,1280]{5,4,3,2,1,0:T(8,128)(2,1)S(1)}, u32[]{:S(2)}, u32[]{:S(2)}) collective-permute-start(bf16[1,1,1,1,72,1280]{5,4,3,2,1,0:T(8,128)(2,1)} %constant_dynamic-slice_fusion.28), channel_id=1, source_target_pairs={{0,16},{2,18},{4,20},{6,22},{8,24},{10,26},{12,28},{14,30},{16,0},... | collective-permute-start | bytes 552968 | tf_op jit(solution)/shard_map/ppermute | solution.py:74
  832.3 17.7 %collective-permute-start.14 = (bf16[2,2,1,2,72,640]{5,4,3,2,1,0:T(8,128)(2,1)S(1)}, bf16[2,2,1,2,72,640]{5,4,3,2,1,0:T(8,128)(2,1)S(1)}, u32[]{:S(2)}, u32[]{:S(2)}) collective-permute-start(bf16[2,2,1,2,72,640]{5,4,3,2,1,0:T(8,128)(2,1)S(1)} %copy-done.86), channel_id=1, source_target_pairs={{0,4},{2,6},{4,0},{6,2},{8,12},{10,14},{12,8},{14,10},{16,20},{18,... | collective-permute-start | bytes 2211848 | tf_op jit(solution)/shard_map/ppermute | solution.py:74
  836.2 19.4 %collective-permute-start.10 = (bf16[2,2,2,1,72,640]{5,4,3,2,1,0:T(8,128)(2,1)S(1)}, bf16[2,2,2,1,72,640]{5,4,3,2,1,0:T(8,128)(2,1)S(1)}, u32[]{:S(2)}, u32[]{:S(2)}) collective-permute-start(bf16[2,2,2,1,72,640]{5,4,3,2,1,0:T(8,128)(2,1)S(1)} %constant_dynamic-slice_fusion.47), channel_id=1, source_target_pairs={{0,2},{2,0},{4,6},{6,4},{8,10},{10,8},{12,14},{14,12},{16,18},{18,... | collective-permute-start | bytes 2211848 | tf_op jit(solution)/shard_map/ppermute | solution.py:74
  851.0 23.8 %collective-permute-start.15 = (bf16[2,2,1,1,72,640]{5,4,3,2,1,0:T(8,128)(2,1)}, bf16[2,2,1,1,72,640]{5,4,3,2,1,0:T(8,128)(2,1)}, u32[]{:S(2)}, u32[]{:S(2)}) collective-permute-start(bf16[2,2,1,1,72,640]{5,4,3,2,1,0:T(8,128)(2,1)} %constant_dynamic-slice_fusion.42), channel_id=1, source_target_pairs={{0,2},{2,0},{4,6},{6,4},{8,10},{10,8},{12,14},{14,12},{16,18},{18,... | collective-permute-start | bytes 1105928 | tf_op jit(solution)/shard_map/ppermute | solution.py:74
  856.9 20.8 %collective-permute-start.11 = (bf16[2,2,1,1,72,640]{5,4,3,2,1,0:T(8,128)(2,1)}, bf16[2,2,1,1,72,640]{5,4,3,2,1,0:T(8,128)(2,1)}, u32[]{:S(2)}, u32[]{:S(2)}) collective-permute-start(bf16[2,2,1,1,72,640]{5,4,3,2,1,0:T(8,128)(2,1)} %constant_dynamic-slice_fusion.46), channel_id=1, source_target_pairs={{0,4},{2,6},{4,0},{6,2},{8,12},{10,14},{12,8},{14,10},{16,20},{18,... | collective-permute-start | bytes 1105928 | tf_op jit(solution)/shard_map/ppermute | solution.py:74
  870.5 19.8 %collective-permute-start.18 = (bf16[2,1,2,2,72,384]{5,4,3,2,1,0:T(8,128)(2,1)S(1)}, bf16[2,1,2,2,72,384]{5,4,3,2,1,0:T(8,128)(2,1)S(1)}, u32[]{:S(2)}, u32[]{:S(2)}) collective-permute-start(bf16[2,1,2,2,72,384]{5,4,3,2,1,0:T(8,128)(2,1)S(1)} %constant_dynamic-slice_fusion.39), channel_id=1, source_target_pairs={{0,8},{2,10},{4,12},{6,14},{8,0},{10,2},{12,4},{14,6},{16,24},{18,... | collective-permute-start | bytes 1327112 | tf_op jit(solution)/shard_map/ppermute | solution.py:74
  878.8 11.8 %collective-permute-start.12 = (bf16[2,1,1,1,72,640]{5,4,3,2,1,0:T(8,128)(2,1)S(1)}, bf16[2,1,1,1,72,640]{5,4,3,2,1,0:T(8,128)(2,1)S(1)}, u32[]{:S(2)}, u32[]{:S(2)}) collective-permute-start(bf16[2,1,1,1,72,640]{5,4,3,2,1,0:T(8,128)(2,1)S(1)} %constant_dynamic-slice_fusion.45), channel_id=1, source_target_pairs={{0,8},{2,10},{4,12},{6,14},{8,0},{10,2},{12,4},{14,6},{16,24},{18,... | collective-permute-start | bytes 552968 | tf_op jit(solution)/shard_map/ppermute | solution.py:74
  886.2 16.1 %collective-permute-start.17 = (bf16[1,1,1,1,72,640]{5,4,3,2,1,0:T(8,128)(2,1)S(1)}, bf16[1,1,1,1,72,640]{5,4,3,2,1,0:T(8,128)(2,1)S(1)}, u32[]{:S(2)}, u32[]{:S(2)}) collective-permute-start(bf16[1,1,1,1,72,640]{5,4,3,2,1,0:T(8,128)(2,1)S(1)} %constant_dynamic-slice_fusion.40), channel_id=1, source_target_pairs={{0,16},{2,18},{4,20},{6,22},{8,24},{10,26},{12,28},{14,30},{16,0},... | collective-permute-start | bytes 276488 | tf_op jit(solution)/shard_map/ppermute | solution.py:74
  890.7 16.5 %collective-permute-start.13 = (bf16[1,1,1,1,72,640]{5,4,3,2,1,0:T(8,128)(2,1)S(1)}, bf16[1,1,1,1,72,640]{5,4,3,2,1,0:T(8,128)(2,1)S(1)}, u32[]{:S(2)}, u32[]{:S(2)}) collective-permute-start(bf16[1,1,1,1,72,640]{5,4,3,2,1,0:T(8,128)(2,1)S(1)} %constant_dynamic-slice_fusion.44), channel_id=1, source_target_pairs={{0,16},{2,18},{4,20},{6,22},{8,24},{10,26},{12,28},{14,30},{16,0},... | collective-permute-start | bytes 276488 | tf_op jit(solution)/shard_map/ppermute | solution.py:74
  (153 other events, 1438.1 us)
Sparse Core Ops, SparseCore 0:
  13.0 75.9 all-gather.4
  91.8 107.5 all-gather.6
  202.1 107.1 all-gather.8
  311.9 107.1 all-gather.10

commit v2 on v1

--- a/solution.py
+++ b/solution.py
@@ -60,7 +60,7 @@
     return terms[:half] + swap_pair(terms[half:].astype(jnp.bfloat16)).astype(jnp.float32)
 
 
-def halving_sum(terms, order):
+def halving_sum(terms, order, after=None):
     count = lax.axis_size("dp")
     place = lax.axis_index("dp")
     bits = len(order)
@@ -73,6 +73,8 @@
         sent = lax.dynamic_slice_in_dim(total, 1 - mine, 1, axis)
         got = lax.ppermute(sent, "dp", [(i, i ^ (1 << bit)) for i in range(count)])
         total = kept.astype(jnp.float32) + got.astype(jnp.float32)
+        if after is not None and bit == order[0]:
+            total = total + after
         if bit != order[-1]:
             total = total.astype(jnp.bfloat16)
     return total.reshape(rows, terms.shape[1])
@@ -99,13 +101,13 @@
     )
 
 
-def grad_scatter(left, right):
+def grad_scatter(left, right, after=None):
     parts = []
     for lo, hi, order in column_plan(right.shape[1]):
         terms = jnp.einsum(
             "td,tf->df", left, right[:, lo:hi], preferred_element_type=jnp.float32
         ).astype(jnp.bfloat16)
-        parts.append(halving_sum(terms, order))
+        parts.append(halving_sum(terms, order, after))
     return jnp.concatenate(parts, axis=1)
 
 
@@ -169,8 +171,11 @@
     gain_query, gain_key = (
         gain_columns[:, i].reshape(count, rows)[:, :head_rows].reshape(-1) for i in (4, 5)
     )
-    gate_weight = lax.all_gather(gate_weight, "dp", axis=0, tiled=True)
-    up_weight = lax.all_gather(up_weight, "dp", axis=0, tiled=True)
+    units = gate_weight.shape[1]
+    gate_up = lax.all_gather(
+        jnp.concatenate([gate_weight, up_weight], axis=1), "dp", axis=0, tiled=True
+    )
+    gate_weight, up_weight = gate_up[:, :units], gate_up[:, units:]
     down_weight = lax.all_gather(down_weight, "dp", axis=0, tiled=True)
     gain_attn_in = gain_attn_in.astype(jnp.float32)
     gain_attn_out = gain_attn_out.astype(jnp.float32)
@@ -243,8 +248,6 @@
     gate_grad, upper_grad = gelu_pull(hidden_grad)
     gate_low = gate_grad.astype(jnp.bfloat16)
     upper_low = upper_grad.astype(jnp.bfloat16)
-    gate_weight_grad = grad_scatter(ffn_inputs, gate_low)
-    up_weight_grad = grad_scatter(ffn_inputs, upper_low)
     ffn_in_terms = jnp.einsum(
         "tf,df->td", gate_low, gate_weight, preferred_element_type=jnp.float32
     ) + jnp.einsum("tf,df->td", upper_low, up_weight, preferred_element_type=jnp.float32)
@@ -280,6 +283,12 @@
     query_raw_grad, gain_query_parts = norm_back(query_turned, query_hat, query_inv, gain_query)
     gain_query_grad = jnp.sum(gain_query_parts, axis=(0, 1))
     query_raw_low = query_raw_grad.reshape(seq_len, local_heads * head_dim).astype(jnp.bfloat16)
+    gate_weight_grad = grad_scatter(
+        ffn_inputs, gate_low, score_grad[0, 0, 0].astype(jnp.float32) * 0.0
+    )
+    up_weight_grad = grad_scatter(
+        ffn_inputs, upper_low, query_raw_low[0, 0].astype(jnp.float32) * 0.0
+    )
     query_weight_grad = jnp.einsum(
         "td,tc->dc", normed_rows, query_raw_low, preferred_element_type=jnp.float32
     )

time: 932 us -> 896 us (0.961)
  starting transfers between devices: 66.9 us -> 45.3 us
  waiting for transfers between devices: 489 us -> 479 us
    ppermute x48, waiting for transfers between devices: 161 us -> 186 us  [halving_sum(): got = lax.ppermute(sent, 'dp', [(i, i ^ 1 << bit) for i in range(count)])]
    ppermute x48, starting transfers between devices: 64.6 us -> 43.3 us  [halving_sum(): got = lax.ppermute(sent, 'dp', [(i, i ^ 1 << bit) for i in range(count)])]
    all_gather x2 -> x1, waiting for transfers between devices: 154 us -> 135 us  [per_device(): lax.all_gather(jnp.concatenate([gate_weight, up_weight], axis=1), 'dp', a...]
    all_gather x1, waiting for transfers between devices: 89.8 us -> 75.1 us  [per_device(): down_weight = lax.all_gather(down_weight, 'dp', axis=0, tiled=True)]
    unnamed x281 -> x319, local copies, waits for them, and re-layouts: 19 us -> 21.6 us
  transfers between devices with their start and end apart: 63 -> 62, of which waited for: 31 -> 32; matrix products, arithmetic and copies ran while one was open for 33% -> 33% of each run, Pallas kernels for 0% -> 0%
where the time goes in v2:
time: 896 us; the launch traced here: 885 us
  waiting for transfers between devices  479 us (53%)
  matrix products  192 us (21%)
  local copies, waits for them, and re-layouts  80 us (9%)
  other arithmetic  71.7 us (8%)
  starting transfers between devices  45.3 us (5%)
  between operations  18 us (2%)
    ppermute x48, waiting for transfers between devices, halving_sum(): got = lax.ppermute(sent, 'dp', [(i, i ^ 1 << bit) for i in range(count)])  186 us
    all_gather x1, waiting for transfers between devices, per_device(): lax.all_gather(jnp.concatenate([gate_weight, up_weight], axis=1), 'dp', a...  135 us
    all_gather x1, waiting for transfers between devices, per_device(): down_weight = lax.all_gather(down_weight, 'dp', axis=0, tiled=True)  75.1 us
    all_gather x1, waiting for transfers between devices, per_device(): packed = lax.all_gather(packed, 'dp', axis=0, tiled=True)  72.6 us
    dot_general x9, matrix products, grad_scatter(): jnp.einsum('td,tf->df', left, right[:, lo:hi], preferred_element_type=jnp...  46.9 us
    ppermute x48, starting transfers between devices, halving_sum(): got = lax.ppermute(sent, 'dp', [(i, i ^ 1 << bit) for i in range(count)])  43.3 us
    dynamic_slice x48, local copies, waits for them, and re-layouts, halving_sum(): sent = lax.dynamic_slice_in_dim(total, 1 - mine, 1, axis)  27.2 us
    convert_element_type x36, other arithmetic, halving_sum(): total = total.astype(jnp.bfloat16)  26.8 us
  transfers between devices with their start and end apart: 62, of which 32 were waited for; matrix products, arithmetic and copies ran while one was open for 33% of the time, Pallas kernels for 0%

profile of v2, /device:TPU:0, one launch (start us, length us, event | category | flops | bytes accessed | tf_op | source)
XLA Modules:
  0.0 885.5 jit_solution(17768520989485137048)
XLA Ops:
  16.5 72.6 %all-gather.4.cloned.1.call-done = bf16[1152,1664]{1,0:T(8,128)(2,1)} async-done(((bf16[72,1664]{1,0:T(8,128)(2,1)}), bf16[1152,1664]{1,0:T(8,128)(2,1)}) %all-gather.4.cloned.1.call-update) | async-done | bytes 3833872 | tf_op jit(solution)/shard_map/all_gather | solution.py:162
  89.1 2.9 convert_reduce_fusion.1
  99.9 3.2 fusion.80
  107.1 4.6 multiply_reduce_fusion.8
  124.8 3.3 fusion.67
  128.1 3.2 fusion.73
  139.3 135.4 %all-gather.6.cloned.1.call-done = bf16[1152,6912]{1,0:T(8,128)(2,1)} async-done(((bf16[72,6912]{1,0:T(8,128)(2,1)}), bf16[1152,6912]{1,0:T(8,128)(2,1)}) %all-gather.6.cloned.1.call-update) | async-done | bytes 15925264 | tf_op jit(solution)/shard_map/all_gather | solution.py:175
  274.7 15.1 %fusion.17 = f32[1024,3456]{1,0:T(8,128)} fusion(bf16[1152,6912]{1,0:T(8,128)(2,1)} %all-gather.6.cloned.1.call-done, bf16[512,1152]{1,0:T(8,128)(2,1)} %collective-permute-done.2, bf16[512,1152]{1,0:T(8,128)(2,1)S(1)} %multiply_convert_fusion.3), kind=kOutput, calls=%fused_computation.34 | convolution fusion | flops 8158445568 | bytes 24477696 | tf_op jit(solution)/shard_map/dot_general | solution.py:233
  289.8 19.7 %multiply_convert_fusion.1 = (bf16[1024,3456]{1,0:T(8,128)(2,1)}, f32[1024,3456]{1,0:T(8,128)}) fusion(f32[1024,3456]{1,0:T(8,128)} %fusion.17, bf16[1152,6912]{1,0:T(8,128)(2,1)} %all-gather.6.cloned.1.call-done, bf16[512,1152]{1,0:T(8,128)(2,1)} %collective-permute-done.2, bf16[512,1152]{1,0:T(8,128)(2,1)S(1)} %multiply_convert_fusion.3), kind=kOutput, calls=%fused_computation.10 | convolution fusion | flops 8193835008 | bytes 45711360 | tf_op jit(solution)/shard_map/dot_general | solution.py:234
  309.5 75.1 %all-gather.8.cloned.1.call-done = bf16[1152,3456]{1,0:T(8,128)(2,1)} async-done(((bf16[72,3456]{1,0:T(8,128)(2,1)}), bf16[1152,3456]{1,0:T(8,128)(2,1)}) %all-gather.8.cloned.1.call-update) | async-done | bytes 7962640 | tf_op jit(solution)/shard_map/all_gather | solution.py:179
  384.6 13.5 %fusion.117 = f32[1024,1152]{1,0:T(8,128)S(1)} fusion(bf16[1024,3456]{1,0:T(8,128)(2,1)} %get-tuple-element.79, bf16[1152,3456]{1,0:T(8,128)(2,1)} %all-gather.8.cloned.1.call-done), kind=kOutput, calls=%fused_computation.345 | convolution fusion | flops 8153726976 | bytes 19759104 | tf_op jit(solution)/shard_map/tf,df->td/dot_general | solution.py:237
  410.2 5.7 convolution_convert_fusion.1
  419.5 5.7 convolution_convert_fusion
  427.1 4.9 convolution_convert_fusion.6
  434.8 25.4 %fusion.6 = (bf16[1024,3456]{1,0:T(8,128)(2,1)}, bf16[1024,3456]{1,0:T(8,128)(2,1)}) fusion(f32[1024,3456]{1,0:T(8,128)} %fusion.17, f32[1024,3456]{1,0:T(8,128)} %get-tuple-element.80, bf16[1152,3456]{1,0:T(8,128)(2,1)} %all-gather.8.cloned.1.call-done, bf16[512,1152]{1,0:T(8,128)(2,1)} %collective-permute-done.4, bf16[512,1152]{1,0:T(8,128)(2,1)} %get-tuple-element.44), kind=kOutput, calls=%fused_computation.8 | convolution fusion | flops 8243380224 | bytes 52789248 | tf_op jit(solution)/shard_map/dot_general | solution.py:247
  460.1 5.5 convolution_convert_fusion.3
  469.9 12.9 %fusion.11 = f32[1024,1152]{1,0:T(8,128)S(1)} fusion(bf16[1024,3456]{1,0:T(8,128)(2,1)S(1)} %copy-done.145, bf16[1152,6912]{1,0:T(8,128)(2,1)} %all-gather.6.cloned.1.call-done), kind=kOutput, calls=%fused_computation.28 | convolution fusion | flops 8153726976 | bytes 19759104 | tf_op jit(solution)/shard_map/tf,df->td/dot_general | solution.py:253
  482.8 14.3 %fusion.21 = f32[1024,1152]{1,0:T(8,128)S(1)} fusion(f32[1024,1152]{1,0:T(8,128)S(1)} %fusion.11, bf16[1024,3456]{1,0:T(8,128)(2,1)} %get-tuple-element.42, bf16[1152,6912]{1,0:T(8,128)(2,1)} %all-gather.6.cloned.1.call-done), kind=kOutput, calls=%fused_computation.40 | convolution fusion | flops 8154906624 | bytes 24477696 | tf_op jit(solution)/shard_map/tf,df->td/dot_general | solution.py:251
  497.4 5.4 convolution_convert_fusion.2
  504.0 6.0 convolution_convert_fusion.7
  511.2 4.6 convolution_convert_fusion.5
  518.6 4.1 convolution_convert_fusion.8
  525.1 5.1 convolution_convert_fusion.4
  545.3 25.2 %collective-permute-done.56 = bf16[1,1,2,2,72,896]{5,4,3,2,1,0:T(8,128)(2,1)S(1)} collective-permute-done((bf16[1,1,2,2,72,896]{5,4,3,2,1,0:T(8,128)(2,1)S(1)}, bf16[1,1,2,2,72,896]{5,4,3,2,1,0:T(8,128)(2,1)S(1)}, u32[]{:S(2)}, u32[]{:S(2)}) %collective-permute-start.56) | collective-permute-done | bytes 516128 | tf_op jit(solution)/shard_map/ppermute | solution.py:74
  574.5 4.4 collective-permute-done.57
  580.6 10.8 %collective-permute-done.58 = bf16[1,1,1,1,72,896]{5,4,3,2,1,0:T(8,128)(2,1)S(1)} collective-permute-done((bf16[1,1,1,1,72,896]{5,4,3,2,1,0:T(8,128)(2,1)S(1)}, bf16[1,1,1,1,72,896]{5,4,3,2,1,0:T(8,128)(2,1)S(1)}, u32[]{:S(2)}, u32[]{:S(2)}) %collective-permute-start.58) | collective-permute-done | bytes 129056 | tf_op jit(solution)/shard_map/ppermute | solution.py:74
  593.7 17.3 %collective-permute-done.52 = bf16[2,2,1,1,72,1280]{5,4,3,2,1,0:T(8,128)(2,1)S(1)} collective-permute-done((bf16[2,2,1,1,72,1280]{5,4,3,2,1,0:T(8,128)(2,1)S(1)}, bf16[2,2,1,1,72,1280]{5,4,3,2,1,0:T(8,128)(2,1)S(1)}, u32[]{:S(2)}, u32[]{:S(2)}) %collective-permute-start.52) | collective-permute-done | bytes 737312 | tf_op jit(solution)/shard_map/ppermute | solution.py:74
  628.2 3.2 copy.104
  655.7 3.0 fusion.75
  674.2 2.9 convolution_convert_fusion.10
  679.5 4.5 collective-permute-done.53
  697.7 3.7 copy.108
  706.7 9.1 %collective-permute-done.54 = bf16[1,1,1,1,72,1280]{5,4,3,2,1,0:T(8,128)(2,1)S(1)} collective-permute-done((bf16[1,1,1,1,72,1280]{5,4,3,2,1,0:T(8,128)(2,1)S(1)}, bf16[1,1,1,1,72,1280]{5,4,3,2,1,0:T(8,128)(2,1)S(1)}, u32[]{:S(2)}, u32[]{:S(2)}) %collective-permute-start.54) | collective-permute-done | bytes 184352 | tf_op jit(solution)/shard_map/ppermute | solution.py:74
  719.9 21.1 %collective-permute-done.32 = bf16[1,1,2,2,72,896]{5,4,3,2,1,0:T(8,128)(2,1)S(1)} collective-permute-done((bf16[1,1,2,2,72,896]{5,4,3,2,1,0:T(8,128)(2,1)}, bf16[1,1,2,2,72,896]{5,4,3,2,1,0:T(8,128)(2,1)S(1)}, u32[]{:S(2)}, u32[]{:S(2)}) %collective-permute-start.32) | collective-permute-done | bytes 516128 | tf_op jit(solution)/shard_map/ppermute | solution.py:74
  750.1 19.0 %collective-permute-done.45 = bf16[1,1,2,1,72,896]{5,4,3,2,1,0:T(8,128)(2,1)S(1)} collective-permute-done((bf16[1,1,2,1,72,896]{5,4,3,2,1,0:T(8,128)(2,1)S(1)}, bf16[1,1,2,1,72,896]{5,4,3,2,1,0:T(8,128)(2,1)S(1)}, u32[]{:S(2)}, u32[]{:S(2)}) %collective-permute-start.45) | collective-permute-done | bytes 258080 | tf_op jit(solution)/shard_map/ppermute | solution.py:74
  769.2 4.7 collective-permute-done.33
  774.5 4.4 collective-permute-done.46
  780.1 3.7 collective-permute-done.34
  790.1 5.3 collective-permute-done.41
  795.9 9.3 %collective-permute-done.25 = bf16[2,1,1,1,72,1280]{5,4,3,2,1,0:T(8,128)(2,1)S(1)} collective-permute-done((bf16[2,1,1,1,72,1280]{5,4,3,2,1,0:T(8,128)(2,1)S(1)}, bf16[2,1,1,1,72,1280]{5,4,3,2,1,0:T(8,128)(2,1)S(1)}, u32[]{:S(2)}, u32[]{:S(2)}) %collective-permute-start.25) | collective-permute-done | bytes 368672 | tf_op jit(solution)/shard_map/ppermute | solution.py:74
  818.9 6.5 collective-permute-done.38
  826.3 3.2 collective-permute-done.42
  831.4 3.7 collective-permute-done.26
  842.5 7.9 collective-permute-done.16
  850.7 3.0 collective-permute-start.19
  854.2 11.7 %collective-permute-done.19 = bf16[1,1,2,2,72,384]{5,4,3,2,1,0:T(8,128)(2,1)S(1)} collective-permute-done((bf16[1,1,2,2,72,384]{5,4,3,2,1,0:T(8,128)(2,1)S(1)}, bf16[1,1,2,2,72,384]{5,4,3,2,1,0:T(8,128)(2,1)S(1)}, u32[]{:S(2)}, u32[]{:S(2)}) %collective-permute-start.19) | collective-permute-done | bytes 221216 | tf_op jit(solution)/shard_map/ppermute | solution.py:74
  866.5 4.2 collective-permute-done.20
  871.4 3.7 collective-permute-done.21
  (634 shorter events, 224.2 us)
Async XLA Ops:
  7.2 81.9 %all-gather.4.cloned.1.call-start = ((), (), s32[]{:S(2)}) async-start(), calls=%async_computation | async-start | bytes 4073472 | tf_op jit(solution)/shard_map/all_gather | solution.py:162
  12.9 261.8 %all-gather.6.cloned.1.call-start = ((), (), s32[]{:S(2)}) async-start(), calls=%async_computation.1 | async-start | bytes 16920576 | tf_op jit(solution)/shard_map/all_gather | solution.py:175
  15.2 369.4 %all-gather.8.cloned.1.call-start = ((), (), s32[]{:S(2)}) async-start(), calls=%async_computation.2 | async-start | bytes 8460288 | tf_op jit(solution)/shard_map/all_gather | solution.py:179
  418.0 123.9 %collective-permute-start.47 = (bf16[2,2,2,1,72,1280]{5,4,3,2,1,0:T(8,128)(2,1)}, bf16[2,2,2,1,72,1280]{5,4,3,2,1,0:T(8,128)(2,1)}, u32[]{:S(2)}, u32[]{:S(2)}) collective-permute-start(bf16[2,2,2,1,72,1280]{5,4,3,2,1,0:T(8,128)(2,1)} %constant_dynamic-slice_fusion.11), channel_id=1, source_target_pairs={{0,2},{2,0},{4,6},{6,4},{8,10},{10,8},{12,14},{14,12},{16,18},{18,... | collective-permute-start | bytes 4423688 | tf_op jit(solution)/shard_map/ppermute | solution.py:74
  426.5 145.1 %collective-permute-start.51 = (bf16[2,2,1,2,72,1280]{5,4,3,2,1,0:T(8,128)(2,1)}, bf16[2,2,1,2,72,1280]{5,4,3,2,1,0:T(8,128)(2,1)}, u32[]{:S(2)}, u32[]{:S(2)}) collective-permute-start(bf16[2,2,1,2,72,1280]{5,4,3,2,1,0:T(8,128)(2,1)} %constant_dynamic-slice_fusion.7), channel_id=1, source_target_pairs={{0,4},{2,6},{4,0},{6,2},{8,12},{10,14},{12,8},{14,10},{16,20},{18,... | collective-permute-start | bytes 4423688 | tf_op jit(solution)/shard_map/ppermute | solution.py:74
  434.3 97.1 %collective-permute-start.55 = (bf16[2,1,2,2,72,896]{5,4,3,2,1,0:T(8,128)(2,1)}, bf16[2,1,2,2,72,896]{5,4,3,2,1,0:T(8,128)(2,1)}, u32[]{:S(2)}, u32[]{:S(2)}) collective-permute-start(bf16[2,1,2,2,72,896]{5,4,3,2,1,0:T(8,128)(2,1)} %constant_dynamic-slice_fusion.3), channel_id=1, source_target_pairs={{0,8},{2,10},{4,12},{6,14},{8,0},{10,2},{12,4},{14,6},{16,24},{18,... | collective-permute-start | bytes 3096584 | tf_op jit(solution)/shard_map/ppermute | solution.py:74
  468.4 167.3 %collective-permute-start.35 = (bf16[2,2,2,1,72,1280]{5,4,3,2,1,0:T(8,128)(2,1)}, bf16[2,2,2,1,72,1280]{5,4,3,2,1,0:T(8,128)(2,1)}, u32[]{:S(2)}, u32[]{:S(2)}) collective-permute-start(bf16[2,2,2,1,72,1280]{5,4,3,2,1,0:T(8,128)(2,1)} %constant_dynamic-slice_fusion.23), channel_id=1, source_target_pairs={{0,2},{2,0},{4,6},{6,4},{8,10},{10,8},{12,14},{14,12},{16,18},{18,... | collective-permute-start | bytes 4423688 | tf_op jit(solution)/shard_map/ppermute | solution.py:74
  497.3 37.6 %collective-permute-start.5 = (bf16[512,1152]{1,0:T(8,128)(2,1)S(1)}, bf16[512,1152]{1,0:T(8,128)(2,1)S(1)}, u32[]{:S(2)}, u32[]{:S(2)}) collective-permute-start(bf16[512,1152]{1,0:T(8,128)(2,1)S(1)} %slice.465), channel_id=1, source_target_pairs={{0,1},{1,0},{2,3},{3,2},{4,5},{5,4},{6,7},{7,6},{8,9},{9,8},{10,11... | collective-permute-start | bytes 3538952 | tf_op jit(solution)/shard_map/ppermute | solution.py:51
  532.4 108.9 %collective-permute-start.39 = (bf16[2,2,1,2,72,1280]{5,4,3,2,1,0:T(8,128)(2,1)}, bf16[2,2,1,2,72,1280]{5,4,3,2,1,0:T(8,128)(2,1)}, u32[]{:S(2)}, u32[]{:S(2)}) collective-permute-start(bf16[2,2,1,2,72,1280]{5,4,3,2,1,0:T(8,128)(2,1)} %constant_dynamic-slice_fusion.19), channel_id=1, source_target_pairs={{0,4},{2,6},{4,0},{6,2},{8,12},{10,14},{12,8},{14,10},{16,20},{18,... | collective-permute-start | bytes 4423688 | tf_op jit(solution)/shard_map/ppermute | solution.py:74
  534.8 115.8 %collective-permute-start.43 = (bf16[2,1,2,2,72,896]{5,4,3,2,1,0:T(8,128)(2,1)}, bf16[2,1,2,2,72,896]{5,4,3,2,1,0:T(8,128)(2,1)}, u32[]{:S(2)}, u32[]{:S(2)}) collective-permute-start(bf16[2,1,2,2,72,896]{5,4,3,2,1,0:T(8,128)(2,1)} %constant_dynamic-slice_fusion.15), channel_id=1, source_target_pairs={{0,8},{2,10},{4,12},{6,14},{8,0},{10,2},{12,4},{14,6},{16,24},{18,... | collective-permute-start | bytes 3096584 | tf_op jit(solution)/shard_map/ppermute | solution.py:74
  541.9 28.6 %collective-permute-start.56 = (bf16[1,1,2,2,72,896]{5,4,3,2,1,0:T(8,128)(2,1)S(1)}, bf16[1,1,2,2,72,896]{5,4,3,2,1,0:T(8,128)(2,1)S(1)}, u32[]{:S(2)}, u32[]{:S(2)}) collective-permute-start(bf16[1,1,2,2,72,896]{5,4,3,2,1,0:T(8,128)(2,1)S(1)} %constant_dynamic-slice_fusion.2), channel_id=1, source_target_pairs={{0,16},{2,18},{4,20},{6,22},{8,24},{10,26},{12,28},{14,30},{16,0},... | collective-permute-start | bytes 1548296 | tf_op jit(solution)/shard_map/ppermute | solution.py:74
  570.5 21.6 %collective-permute-start.48 = (bf16[2,2,1,1,72,1280]{5,4,3,2,1,0:T(8,128)(2,1)S(1)}, bf16[2,2,1,1,72,1280]{5,4,3,2,1,0:T(8,128)(2,1)S(1)}, u32[]{:S(2)}, u32[]{:S(2)}) collective-permute-start(bf16[2,2,1,1,72,1280]{5,4,3,2,1,0:T(8,128)(2,1)S(1)} %constant_dynamic-slice_fusion.10), channel_id=1, source_target_pairs={{0,4},{2,6},{4,0},{6,2},{8,12},{10,14},{12,8},{14,10},{16,20},{18,... | collective-permute-start | bytes 2211848 | tf_op jit(solution)/shard_map/ppermute | solution.py:74
  579.0 12.4 %collective-permute-start.58 = (bf16[1,1,1,1,72,896]{5,4,3,2,1,0:T(8,128)(2,1)S(1)}, bf16[1,1,1,1,72,896]{5,4,3,2,1,0:T(8,128)(2,1)S(1)}, u32[]{:S(2)}, u32[]{:S(2)}) collective-permute-start(bf16[1,1,1,1,72,896]{5,4,3,2,1,0:T(8,128)(2,1)S(1)} %constant_dynamic-slice_fusion), channel_id=1, source_target_pairs={{0,4},{2,6},{4,0},{6,2},{8,12},{10,14},{12,8},{14,10},{16,20},{18,... | collective-permute-start | bytes 387080 | tf_op jit(solution)/shard_map/ppermute | solution.py:74
  591.4 21.4 %collective-permute-start.6 = (bf16[512,1152]{1,0:T(8,128)(2,1)S(1)}, bf16[512,1152]{1,0:T(8,128)(2,1)S(1)}, u32[]{:S(2)}, u32[]{:S(2)}) collective-permute-start(bf16[512,1152]{1,0:T(8,128)(2,1)S(1)} %multiply_convert_fusion.2), channel_id=1, source_target_pairs={{0,1},{1,0},{2,3},{3,2},{4,5},{5,4},{6,7},{7,6},{8,9},{9,8},{10,11... | collective-permute-start | bytes 3538952 | tf_op jit(solution)/shard_map/ppermute | solution.py:51
  592.1 18.9 %collective-permute-start.52 = (bf16[2,2,1,1,72,1280]{5,4,3,2,1,0:T(8,128)(2,1)S(1)}, bf16[2,2,1,1,72,1280]{5,4,3,2,1,0:T(8,128)(2,1)S(1)}, u32[]{:S(2)}, u32[]{:S(2)}) collective-permute-start(bf16[2,2,1,1,72,1280]{5,4,3,2,1,0:T(8,128)(2,1)S(1)} %constant_dynamic-slice_fusion.6), channel_id=1, source_target_pairs={{0,2},{2,0},{4,6},{6,4},{8,10},{10,8},{12,14},{14,12},{16,18},{18,... | collective-permute-start | bytes 2211848 | tf_op jit(solution)/shard_map/ppermute | solution.py:74
  611.0 34.2 %collective-permute-start.23 = (bf16[2,2,2,1,72,1280]{5,4,3,2,1,0:T(8,128)(2,1)}, bf16[2,2,2,1,72,1280]{5,4,3,2,1,0:T(8,128)(2,1)}, u32[]{:S(2)}, u32[]{:S(2)}) collective-permute-start(bf16[2,2,2,1,72,1280]{5,4,3,2,1,0:T(8,128)(2,1)} %constant_dynamic-slice_fusion.35), channel_id=1, source_target_pairs={{0,2},{2,0},{4,6},{6,4},{8,10},{10,8},{12,14},{14,12},{16,18},{18,... | collective-permute-start | bytes 4423688 | tf_op jit(solution)/shard_map/ppermute | solution.py:74
  612.8 47.4 %collective-permute-start.27 = (bf16[2,2,1,2,72,1280]{5,4,3,2,1,0:T(8,128)(2,1)}, bf16[2,2,1,2,72,1280]{5,4,3,2,1,0:T(8,128)(2,1)}, u32[]{:S(2)}, u32[]{:S(2)}) collective-permute-start(bf16[2,2,1,2,72,1280]{5,4,3,2,1,0:T(8,128)(2,1)} %constant_dynamic-slice_fusion.31), channel_id=1, source_target_pairs={{0,4},{2,6},{4,0},{6,2},{8,12},{10,14},{12,8},{14,10},{16,20},{18,... | collective-permute-start | bytes 4423688 | tf_op jit(solution)/shard_map/ppermute | solution.py:74
  635.7 33.1 %collective-permute-start.31 = (bf16[2,1,2,2,72,896]{5,4,3,2,1,0:T(8,128)(2,1)S(1)}, bf16[2,1,2,2,72,896]{5,4,3,2,1,0:T(8,128)(2,1)S(1)}, u32[]{:S(2)}, u32[]{:S(2)}) collective-permute-start(bf16[2,1,2,2,72,896]{5,4,3,2,1,0:T(8,128)(2,1)S(1)} %copy-done.98), channel_id=1, source_target_pairs={{0,8},{2,10},{4,12},{6,14},{8,0},{10,2},{12,4},{14,6},{16,24},{18,... | collective-permute-start | bytes 3096584 | tf_op jit(solution)/shard_map/ppermute | solution.py:74
  641.3 35.9 %collective-permute-start.49 = (bf16[2,1,1,1,72,1280]{5,4,3,2,1,0:T(8,128)(2,1)}, bf16[2,1,1,1,72,1280]{5,4,3,2,1,0:T(8,128)(2,1)}, u32[]{:S(2)}, u32[]{:S(2)}) collective-permute-start(bf16[2,1,1,1,72,1280]{5,4,3,2,1,0:T(8,128)(2,1)} %constant_dynamic-slice_fusion.9), channel_id=1, source_target_pairs={{0,8},{2,10},{4,12},{6,14},{8,0},{10,2},{12,4},{14,6},{16,24},{18,... | collective-permute-start | bytes 1105928 | tf_op jit(solution)/shard_map/ppermute | solution.py:74
  645.3 38.7 %collective-permute-start.53 = (bf16[2,1,1,1,72,1280]{5,4,3,2,1,0:T(8,128)(2,1)}, bf16[2,1,1,1,72,1280]{5,4,3,2,1,0:T(8,128)(2,1)}, u32[]{:S(2)}, u32[]{:S(2)}) collective-permute-start(bf16[2,1,1,1,72,1280]{5,4,3,2,1,0:T(8,128)(2,1)} %constant_dynamic-slice_fusion.5), channel_id=1, source_target_pairs={{0,8},{2,10},{4,12},{6,14},{8,0},{10,2},{12,4},{14,6},{16,24},{18,... | collective-permute-start | bytes 1105928 | tf_op jit(solution)/shard_map/ppermute | solution.py:74
  650.7 90.5 %collective-permute-start.36 = (bf16[2,2,1,1,72,1280]{5,4,3,2,1,0:T(8,128)(2,1)}, bf16[2,2,1,1,72,1280]{5,4,3,2,1,0:T(8,128)(2,1)}, u32[]{:S(2)}, u32[]{:S(2)}) collective-permute-start(bf16[2,2,1,1,72,1280]{5,4,3,2,1,0:T(8,128)(2,1)} %constant_dynamic-slice_fusion.22), channel_id=1, source_target_pairs={{0,4},{2,6},{4,0},{6,2},{8,12},{10,14},{12,8},{14,10},{16,20},{18,... | collective-permute-start | bytes 2211848 | tf_op jit(solution)/shard_map/ppermute | solution.py:74
  660.2 84.0 %collective-permute-start.40 = (bf16[2,2,1,1,72,1280]{5,4,3,2,1,0:T(8,128)(2,1)}, bf16[2,2,1,1,72,1280]{5,4,3,2,1,0:T(8,128)(2,1)}, u32[]{:S(2)}, u32[]{:S(2)}) collective-permute-start(bf16[2,2,1,1,72,1280]{5,4,3,2,1,0:T(8,128)(2,1)} %constant_dynamic-slice_fusion.18), channel_id=1, source_target_pairs={{0,2},{2,0},{4,6},{6,4},{8,10},{10,8},{12,14},{14,12},{16,18},{18,... | collective-permute-start | bytes 2211848 | tf_op jit(solution)/shard_map/ppermute | solution.py:74
  668.8 48.1 %collective-permute-start.44 = (bf16[1,1,2,2,72,896]{5,4,3,2,1,0:T(8,128)(2,1)}, bf16[1,1,2,2,72,896]{5,4,3,2,1,0:T(8,128)(2,1)}, u32[]{:S(2)}, u32[]{:S(2)}) collective-permute-start(bf16[1,1,2,2,72,896]{5,4,3,2,1,0:T(8,128)(2,1)} %constant_dynamic-slice_fusion.14), channel_id=1, source_target_pairs={{0,16},{2,18},{4,20},{6,22},{8,24},{10,26},{12,28},{14,30},{16,0},... | collective-permute-start | bytes 1548296 | tf_op jit(solution)/shard_map/ppermute | solution.py:74
  677.2 69.2 %collective-permute-start.24 = (bf16[2,2,1,1,72,1280]{5,4,3,2,1,0:T(8,128)(2,1)}, bf16[2,2,1,1,72,1280]{5,4,3,2,1,0:T(8,128)(2,1)}, u32[]{:S(2)}, u32[]{:S(2)}) collective-permute-start(bf16[2,2,1,1,72,1280]{5,4,3,2,1,0:T(8,128)(2,1)} %constant_dynamic-slice_fusion.34), channel_id=1, source_target_pairs={{0,4},{2,6},{4,0},{6,2},{8,12},{10,14},{12,8},{14,10},{16,20},{18,... | collective-permute-start | bytes 2211848 | tf_op jit(solution)/shard_map/ppermute | solution.py:74
  704.9 11.0 %collective-permute-start.54 = (bf16[1,1,1,1,72,1280]{5,4,3,2,1,0:T(8,128)(2,1)S(1)}, bf16[1,1,1,1,72,1280]{5,4,3,2,1,0:T(8,128)(2,1)S(1)}, u32[]{:S(2)}, u32[]{:S(2)}) collective-permute-start(bf16[1,1,1,1,72,1280]{5,4,3,2,1,0:T(8,128)(2,1)S(1)} %copy-done.110), channel_id=1, source_target_pairs={{0,16},{2,18},{4,20},{6,22},{8,24},{10,26},{12,28},{14,30},{16,0},... | collective-permute-start | bytes 552968 | tf_op jit(solution)/shard_map/ppermute | solution.py:74
  715.8 25.1 %collective-permute-start.32 = (bf16[1,1,2,2,72,896]{5,4,3,2,1,0:T(8,128)(2,1)}, bf16[1,1,2,2,72,896]{5,4,3,2,1,0:T(8,128)(2,1)S(1)}, u32[]{:S(2)}, u32[]{:S(2)}) collective-permute-start(bf16[1,1,2,2,72,896]{5,4,3,2,1,0:T(8,128)(2,1)} %constant_dynamic-slice_fusion.26), channel_id=1, source_target_pairs={{0,16},{2,18},{4,20},{6,22},{8,24},{10,26},{12,28},{14,30},{16,0},... | collective-permute-start | bytes 1548296 | tf_op jit(solution)/shard_map/ppermute | solution.py:74
  716.9 32.1 %collective-permute-start.28 = (bf16[2,2,1,1,72,1280]{5,4,3,2,1,0:T(8,128)(2,1)S(1)}, bf16[2,2,1,1,72,1280]{5,4,3,2,1,0:T(8,128)(2,1)S(1)}, u32[]{:S(2)}, u32[]{:S(2)}) collective-permute-start(bf16[2,2,1,1,72,1280]{5,4,3,2,1,0:T(8,128)(2,1)S(1)} %copy-done.99), channel_id=1, source_target_pairs={{0,2},{2,0},{4,6},{6,4},{8,10},{10,8},{12,14},{14,12},{16,18},{18,... | collective-permute-start | bytes 2211848 | tf_op jit(solution)/shard_map/ppermute | solution.py:74
  741.0 70.8 %collective-permute-start.7 = (bf16[512,1152]{1,0:T(8,128)(2,1)S(1)}, bf16[512,1152]{1,0:T(8,128)(2,1)S(1)}, u32[]{:S(2)}, u32[]{:S(2)}) collective-permute-start(bf16[512,1152]{1,0:T(8,128)(2,1)S(1)} %copy-done.83), channel_id=1, source_target_pairs={{0,1},{1,0},{2,3},{3,2},{4,5},{5,4},{6,7},{7,6},{8,9},{9,8},{10,11... | collective-permute-start | bytes 3538952 | tf_op jit(solution)/shard_map/ppermute | solution.py:51
  741.2 43.4 %collective-permute-start.14 = (bf16[2,2,1,2,72,640]{5,4,3,2,1,0:T(8,128)(2,1)S(1)}, bf16[2,2,1,2,72,640]{5,4,3,2,1,0:T(8,128)(2,1)S(1)}, u32[]{:S(2)}, u32[]{:S(2)}) collective-permute-start(bf16[2,2,1,2,72,640]{5,4,3,2,1,0:T(8,128)(2,1)S(1)} %copy-done.100), channel_id=1, source_target_pairs={{0,4},{2,6},{4,0},{6,2},{8,12},{10,14},{12,8},{14,10},{16,20},{18,... | collective-permute-start | bytes 2211848 | tf_op jit(solution)/shard_map/ppermute | solution.py:74
  744.2 43.4 %collective-permute-start.10 = (bf16[2,2,2,1,72,640]{5,4,3,2,1,0:T(8,128)(2,1)S(1)}, bf16[2,2,2,1,72,640]{5,4,3,2,1,0:T(8,128)(2,1)S(1)}, u32[]{:S(2)}, u32[]{:S(2)}) collective-permute-start(bf16[2,2,2,1,72,640]{5,4,3,2,1,0:T(8,128)(2,1)S(1)} %constant_dynamic-slice_fusion.47), channel_id=1, source_target_pairs={{0,2},{2,0},{4,6},{6,4},{8,10},{10,8},{12,14},{14,12},{16,18},{18,... | collective-permute-start | bytes 2211848 | tf_op jit(solution)/shard_map/ppermute | solution.py:74
  746.3 22.8 %collective-permute-start.45 = (bf16[1,1,2,1,72,896]{5,4,3,2,1,0:T(8,128)(2,1)S(1)}, bf16[1,1,2,1,72,896]{5,4,3,2,1,0:T(8,128)(2,1)S(1)}, u32[]{:S(2)}, u32[]{:S(2)}) collective-permute-start(bf16[1,1,2,1,72,896]{5,4,3,2,1,0:T(8,128)(2,1)S(1)} %constant_dynamic-slice_fusion.13), channel_id=1, source_target_pairs={{0,2},{2,0},{4,6},{6,4},{8,10},{10,8},{12,14},{14,12},{16,18},{18,... | collective-permute-start | bytes 774152 | tf_op jit(solution)/shard_map/ppermute | solution.py:74
  749.0 24.9 %collective-permute-start.33 = (bf16[1,1,2,1,72,896]{5,4,3,2,1,0:T(8,128)(2,1)S(1)}, bf16[1,1,2,1,72,896]{5,4,3,2,1,0:T(8,128)(2,1)S(1)}, u32[]{:S(2)}, u32[]{:S(2)}) collective-permute-start(bf16[1,1,2,1,72,896]{5,4,3,2,1,0:T(8,128)(2,1)S(1)} %constant_dynamic-slice_fusion.25), channel_id=1, source_target_pairs={{0,2},{2,0},{4,6},{6,4},{8,10},{10,8},{12,14},{14,12},{16,18},{18,... | collective-permute-start | bytes 774152 | tf_op jit(solution)/shard_map/ppermute | solution.py:74
  769.1 19.6 %collective-permute-start.37 = (bf16[2,1,1,1,72,1280]{5,4,3,2,1,0:T(8,128)(2,1)S(1)}, bf16[2,1,1,1,72,1280]{5,4,3,2,1,0:T(8,128)(2,1)S(1)}, u32[]{:S(2)}, u32[]{:S(2)}) collective-permute-start(bf16[2,1,1,1,72,1280]{5,4,3,2,1,0:T(8,128)(2,1)S(1)} %constant_dynamic-slice_fusion.21), channel_id=1, source_target_pairs={{0,8},{2,10},{4,12},{6,14},{8,0},{10,2},{12,4},{14,6},{16,24},{18,... | collective-permute-start | bytes 1105928 | tf_op jit(solution)/shard_map/ppermute | solution.py:74
  783.8 11.5 %collective-permute-start.41 = (bf16[2,1,1,1,72,1280]{5,4,3,2,1,0:T(8,128)(2,1)S(1)}, bf16[2,1,1,1,72,1280]{5,4,3,2,1,0:T(8,128)(2,1)S(1)}, u32[]{:S(2)}, u32[]{:S(2)}) collective-permute-start(bf16[2,1,1,1,72,1280]{5,4,3,2,1,0:T(8,128)(2,1)S(1)} %constant_dynamic-slice_fusion.17), channel_id=1, source_target_pairs={{0,8},{2,10},{4,12},{6,14},{8,0},{10,2},{12,4},{14,6},{16,24},{18,... | collective-permute-start | bytes 1105928 | tf_op jit(solution)/shard_map/ppermute | solution.py:74
  784.6 20.6 %collective-permute-start.25 = (bf16[2,1,1,1,72,1280]{5,4,3,2,1,0:T(8,128)(2,1)S(1)}, bf16[2,1,1,1,72,1280]{5,4,3,2,1,0:T(8,128)(2,1)S(1)}, u32[]{:S(2)}, u32[]{:S(2)}) collective-permute-start(bf16[2,1,1,1,72,1280]{5,4,3,2,1,0:T(8,128)(2,1)S(1)} %constant_dynamic-slice_fusion.33), channel_id=1, source_target_pairs={{0,8},{2,10},{4,12},{6,14},{8,0},{10,2},{12,4},{14,6},{16,24},{18,... | collective-permute-start | bytes 1105928 | tf_op jit(solution)/shard_map/ppermute | solution.py:74
  787.6 21.9 %collective-permute-start.29 = (bf16[2,1,1,1,72,1280]{5,4,3,2,1,0:T(8,128)(2,1)S(1)}, bf16[2,1,1,1,72,1280]{5,4,3,2,1,0:T(8,128)(2,1)S(1)}, u32[]{:S(2)}, u32[]{:S(2)}) collective-permute-start(bf16[2,1,1,1,72,1280]{5,4,3,2,1,0:T(8,128)(2,1)S(1)} %constant_dynamic-slice_fusion.29), channel_id=1, source_target_pairs={{0,8},{2,10},{4,12},{6,14},{8,0},{10,2},{12,4},{14,6},{16,24},{18,... | collective-permute-start | bytes 1105928 | tf_op jit(solution)/shard_map/ppermute | solution.py:74
  788.7 49.4 %collective-permute-start.15 = (bf16[2,2,1,1,72,640]{5,4,3,2,1,0:T(8,128)(2,1)}, bf16[2,2,1,1,72,640]{5,4,3,2,1,0:T(8,128)(2,1)}, u32[]{:S(2)}, u32[]{:S(2)}) collective-permute-start(bf16[2,2,1,1,72,640]{5,4,3,2,1,0:T(8,128)(2,1)} %constant_dynamic-slice_fusion.42), channel_id=1, source_target_pairs={{0,2},{2,0},{4,6},{6,4},{8,10},{10,8},{12,14},{14,12},{16,18},{18,... | collective-permute-start | bytes 1105928 | tf_op jit(solution)/shard_map/ppermute | solution.py:74
  795.3 43.9 %collective-permute-start.11 = (bf16[2,2,1,1,72,640]{5,4,3,2,1,0:T(8,128)(2,1)}, bf16[2,2,1,1,72,640]{5,4,3,2,1,0:T(8,128)(2,1)}, u32[]{:S(2)}, u32[]{:S(2)}) collective-permute-start(bf16[2,2,1,1,72,640]{5,4,3,2,1,0:T(8,128)(2,1)} %constant_dynamic-slice_fusion.46), channel_id=1, source_target_pairs={{0,4},{2,6},{4,0},{6,2},{8,12},{10,14},{12,8},{14,10},{16,20},{18,... | collective-permute-start | bytes 1105928 | tf_op jit(solution)/shard_map/ppermute | solution.py:74
  805.2 20.1 %collective-permute-start.38 = (bf16[1,1,1,1,72,1280]{5,4,3,2,1,0:T(8,128)(2,1)}, bf16[1,1,1,1,72,1280]{5,4,3,2,1,0:T(8,128)(2,1)}, u32[]{:S(2)}, u32[]{:S(2)}) collective-permute-start(bf16[1,1,1,1,72,1280]{5,4,3,2,1,0:T(8,128)(2,1)} %constant_dynamic-slice_fusion.20), channel_id=1, source_target_pairs={{0,16},{2,18},{4,20},{6,22},{8,24},{10,26},{12,28},{14,30},{16,0},... | collective-permute-start | bytes 552968 | tf_op jit(solution)/shard_map/ppermute | solution.py:74
  809.5 20.0 %collective-permute-start.42 = (bf16[1,1,1,1,72,1280]{5,4,3,2,1,0:T(8,128)(2,1)}, bf16[1,1,1,1,72,1280]{5,4,3,2,1,0:T(8,128)(2,1)}, u32[]{:S(2)}, u32[]{:S(2)}) collective-permute-start(bf16[1,1,1,1,72,1280]{5,4,3,2,1,0:T(8,128)(2,1)} %constant_dynamic-slice_fusion.16), channel_id=1, source_target_pairs={{0,16},{2,18},{4,20},{6,22},{8,24},{10,26},{12,28},{14,30},{16,0},... | collective-permute-start | bytes 552968 | tf_op jit(solution)/shard_map/ppermute | solution.py:74
  811.8 23.4 %collective-permute-start.26 = (bf16[1,1,1,1,72,1280]{5,4,3,2,1,0:T(8,128)(2,1)}, bf16[1,1,1,1,72,1280]{5,4,3,2,1,0:T(8,128)(2,1)}, u32[]{:S(2)}, u32[]{:S(2)}) collective-permute-start(bf16[1,1,1,1,72,1280]{5,4,3,2,1,0:T(8,128)(2,1)} %constant_dynamic-slice_fusion.32), channel_id=1, source_target_pairs={{0,16},{2,18},{4,20},{6,22},{8,24},{10,26},{12,28},{14,30},{16,0},... | collective-permute-start | bytes 552968 | tf_op jit(solution)/shard_map/ppermute | solution.py:74
  825.3 11.7 %collective-permute-start.30 = (bf16[1,1,1,1,72,1280]{5,4,3,2,1,0:T(8,128)(2,1)}, bf16[1,1,1,1,72,1280]{5,4,3,2,1,0:T(8,128)(2,1)S(1)}, u32[]{:S(2)}, u32[]{:S(2)}) collective-permute-start(bf16[1,1,1,1,72,1280]{5,4,3,2,1,0:T(8,128)(2,1)} %constant_dynamic-slice_fusion.28), channel_id=1, source_target_pairs={{0,16},{2,18},{4,20},{6,22},{8,24},{10,26},{12,28},{14,30},{16,0},... | collective-permute-start | bytes 552968 | tf_op jit(solution)/shard_map/ppermute | solution.py:74
  829.4 21.1 %collective-permute-start.18 = (bf16[2,1,2,2,72,384]{5,4,3,2,1,0:T(8,128)(2,1)S(1)}, bf16[2,1,2,2,72,384]{5,4,3,2,1,0:T(8,128)(2,1)S(1)}, u32[]{:S(2)}, u32[]{:S(2)}) collective-permute-start(bf16[2,1,2,2,72,384]{5,4,3,2,1,0:T(8,128)(2,1)S(1)} %constant_dynamic-slice_fusion.39), channel_id=1, source_target_pairs={{0,8},{2,10},{4,12},{6,14},{8,0},{10,2},{12,4},{14,6},{16,24},{18,... | collective-permute-start | bytes 1327112 | tf_op jit(solution)/shard_map/ppermute | solution.py:74
  839.2 11.2 %collective-permute-start.16 = (bf16[2,1,1,1,72,640]{5,4,3,2,1,0:T(8,128)(2,1)S(1)}, bf16[2,1,1,1,72,640]{5,4,3,2,1,0:T(8,128)(2,1)S(1)}, u32[]{:S(2)}, u32[]{:S(2)}) collective-permute-start(bf16[2,1,1,1,72,640]{5,4,3,2,1,0:T(8,128)(2,1)S(1)} %constant_dynamic-slice_fusion.41), channel_id=1, source_target_pairs={{0,8},{2,10},{4,12},{6,14},{8,0},{10,2},{12,4},{14,6},{16,24},{18,... | collective-permute-start | bytes 552968 | tf_op jit(solution)/shard_map/ppermute | solution.py:74
  840.4 13.6 %collective-permute-start.12 = (bf16[2,1,1,1,72,640]{5,4,3,2,1,0:T(8,128)(2,1)S(1)}, bf16[2,1,1,1,72,640]{5,4,3,2,1,0:T(8,128)(2,1)S(1)}, u32[]{:S(2)}, u32[]{:S(2)}) collective-permute-start(bf16[2,1,1,1,72,640]{5,4,3,2,1,0:T(8,128)(2,1)S(1)} %constant_dynamic-slice_fusion.45), channel_id=1, source_target_pairs={{0,8},{2,10},{4,12},{6,14},{8,0},{10,2},{12,4},{14,6},{16,24},{18,... | collective-permute-start | bytes 552968 | tf_op jit(solution)/shard_map/ppermute | solution.py:74
  850.5 16.0 %collective-permute-start.17 = (bf16[1,1,1,1,72,640]{5,4,3,2,1,0:T(8,128)(2,1)S(1)}, bf16[1,1,1,1,72,640]{5,4,3,2,1,0:T(8,128)(2,1)S(1)}, u32[]{:S(2)}, u32[]{:S(2)}) collective-permute-start(bf16[1,1,1,1,72,640]{5,4,3,2,1,0:T(8,128)(2,1)S(1)} %constant_dynamic-slice_fusion.40), channel_id=1, source_target_pairs={{0,16},{2,18},{4,20},{6,22},{8,24},{10,26},{12,28},{14,30},{16,0},... | collective-permute-start | bytes 276488 | tf_op jit(solution)/shard_map/ppermute | solution.py:74
  850.7 15.1 %collective-permute-start.19 = (bf16[1,1,2,2,72,384]{5,4,3,2,1,0:T(8,128)(2,1)S(1)}, bf16[1,1,2,2,72,384]{5,4,3,2,1,0:T(8,128)(2,1)S(1)}, u32[]{:S(2)}, u32[]{:S(2)}) collective-permute-start(bf16[1,1,2,2,72,384]{5,4,3,2,1,0:T(8,128)(2,1)S(1)} %constant_dynamic-slice_fusion.38), channel_id=1, source_target_pairs={{0,16},{2,18},{4,20},{6,22},{8,24},{10,26},{12,28},{14,30},{16,0},... | collective-permute-start | bytes 663560 | tf_op jit(solution)/shard_map/ppermute | solution.py:74
  854.1 17.2 %collective-permute-start.13 = (bf16[1,1,1,1,72,640]{5,4,3,2,1,0:T(8,128)(2,1)S(1)}, bf16[1,1,1,1,72,640]{5,4,3,2,1,0:T(8,128)(2,1)S(1)}, u32[]{:S(2)}, u32[]{:S(2)}) collective-permute-start(bf16[1,1,1,1,72,640]{5,4,3,2,1,0:T(8,128)(2,1)S(1)} %constant_dynamic-slice_fusion.44), channel_id=1, source_target_pairs={{0,16},{2,18},{4,20},{6,22},{8,24},{10,26},{12,28},{14,30},{16,0},... | collective-permute-start | bytes 276488 | tf_op jit(solution)/shard_map/ppermute | solution.py:74
  (171 other events, 1797.0 us)
Sparse Core Ops, SparseCore 0:
  13.0 75.9 all-gather.3
  92.4 182.1 all-gather.5
  277.4 107.1 all-gather.7
